TPU v7x, 32 devices: a whole 2x2x4 slice. The times are simulated.
32 devices in a mesh: mem: 4 (over y, x), grid: 8 (over z, core).
Axes of the slice: x: 2, y: 2, z: 4, core: 2. Of those that a mesh axis runs over, the one named last changes fastest.
Arguments:
- ensemble: bfloat16 [1024, 128, 1024], P(('mem', 'grid')), may hold values from -6 to 6
- right_side: float32 [128, 1024], P(('mem', 'grid')), may hold values from -18 to 18
- obs_prec: float32 [128, 1024], P(('mem', 'grid')), may hold values from 0.5 to 2
- neighbors: int32 [128, 8], replicated, may hold values from 0 to 127, as said below
- loc_weight: float32 [128, 8], replicated, may hold values from 0 to 0.08
Outputs:
- solution_field: float32 [128, 1024], P(('mem', 'grid'))
- residual: float32 [128, 1024], P(('mem', 'grid'))
Inputs may be any that keep to these rules, and one draw needn't show every extreme that they name: neighbors[b, j] lies within 3 of b along the cyclic order of blocks, and every block is listed exactly once in each of the 8 columns.
All inputs are finite; a program needn't handle non-finite values.
Results may differ from a plain program's by a relative error of at most 0.0073.
Values may be sent and summed in bfloat16 or wider, within the bound.
No kernel may reach another device: no remote copies, remote signals or barrier semaphores. Data moves between devices by JAX's collectives and lax.ppermute only.
A program may use at most 128 MiB of HBM per device.

v0:
```python
import jax
import jax.numpy as jnp
from jax import lax
from jax.sharding import PartitionSpec as P

M = 1024
ITERS = 2


def with_halo(x, sides, width):
    for axis, dim in sides:
        peers, length = (lax.axis_size(axis), x.shape[dim])
        up = [(i, (i + 1) % peers) for i in range(peers)]
        down = [(j, i) for i, j in up]
        last = lax.slice_in_dim(x, length - width, length, axis=dim)
        first = lax.slice_in_dim(x, 0, width, axis=dim)
        before = lax.ppermute(last, axis, up)
        after = lax.ppermute(first, axis, down)
        x = jnp.concatenate([before, x, after], axis=dim)
    return x


def per_device(ensemble, right_side, obs_prec, neighbors, loc_weight):
    blocks = right_side.shape[0]
    cells = right_side.shape[1]
    total = blocks * lax.axis_size(("mem", "grid"))
    scale = 1.0 / M
    n_mem = lax.axis_size("mem")
    n_grid = lax.axis_size("grid")
    sectioned = ensemble.reshape(ensemble.shape[0], n_mem, n_grid, blocks, cells)
    moved = lax.all_to_all(
        lax.all_to_all(sectioned, "mem", split_axis=1, concat_axis=0, tiled=True),
        "grid",
        split_axis=2,
        concat_axis=0,
        tiled=True,
    )
    relaid = moved.reshape(M, blocks, cells)
    index = lax.axis_index(("mem", "grid"))
    own_nbr = lax.dynamic_slice_in_dim(neighbors, index * blocks, blocks, 0)
    own_weight = lax.dynamic_slice_in_dim(loc_weight, index * blocks, blocks, 0)
    position = (own_nbr - (index - 1) * blocks) % total
    window = jnp.arange(3 * blocks, dtype=jnp.int32)
    mixing = jnp.sum(
        jnp.where(position[:, :, None] == window[None, None, :], own_weight[:, :, None], 0.0),
        axis=1,
    )
    itself = window[None, :] == (blocks + jnp.arange(blocks, dtype=jnp.int32))[:, None]
    mixing = mixing + itself.astype(jnp.float32)
    solution_field = jnp.zeros_like(right_side)
    residual = right_side
    direction = right_side

    def squares(field):
        return lax.psum(jnp.sum(field * field), ("mem", "grid"))

    norm_now = squares(residual)
    for step in range(ITERS):
        rounded = direction.astype(jnp.bfloat16)
        sums = jnp.einsum("mbc,bc->bm", relaid, rounded, preferred_element_type=jnp.float32)
        wider = with_halo(sums, ((("mem", "grid"), 0),), blocks)
        coeff = jnp.dot(
            mixing, wider, precision=lax.Precision.HIGHEST, preferred_element_type=jnp.float32
        ).astype(jnp.bfloat16)
        spread = jnp.einsum("mbc,bm->bc", relaid, coeff, preferred_element_type=jnp.float32)
        image = obs_prec * direction + spread * scale
        alpha = norm_now / lax.psum(jnp.sum(direction * image), ("mem", "grid"))
        solution_field = solution_field + alpha * direction
        residual = residual - alpha * image
        if step + 1 < ITERS:
            norm_next = squares(residual)
            direction = residual + norm_next / norm_now * direction
            norm_now = norm_next
    return (solution_field, residual)


def solution(mesh):
    return jax.shard_map(
        per_device,
        mesh=mesh,
        in_specs=(
            P(("mem", "grid"), None, None),
            P(("mem", "grid"), None),
            P(("mem", "grid"), None),
            P(),
            P(),
        ),
        out_specs=(P(("mem", "grid"), None), P(("mem", "grid"), None)),
        check_vma=False,
    )
```

profile of v0, /device:TPU:1, one launch (start us, length us, event | category | flops | bytes accessed | tf_op | source)
XLA Modules:
  0.0 492.7 jit_solution(10499496195349163883)
XLA Ops:
  0.6 11.3 %copy.25 = bf16[32,128,1024]{2,0,1:T(8,128)(2,1)} copy(bf16[32,128,1024]{2,1,0:T(8,128)(2,1)} %param.5) | data formatting | bytes 16777216 | tf_op args[0]
  11.9 100.3 %all_to_all.33 = bf16[32,4,8,4,1024]{4,0,3,2,1:T(8,128)(2,1)} all-to-all(bf16[32,4,8,4,1024]{4,0,3,2,1:T(8,128)(2,1)} %bitcast.51), channel_id=1, replica_groups=mesh['mem'=4,'grid'=8] {'mem'}, dimensions={1} | all-to-all | bytes 16777216 | tf_op jit(solution)/shard_map/all_to_all | solution.py:32
  112.2 11.4 %copy.26 = bf16[4,32,1,8,4,1024]{5,3,4,2,1,0:T(8,128)(2,1)} copy(bf16[4,32,1,8,4,1024]{5,1,4,3,0,2:T(8,128)(2,1)} %bitcast.49) | data formatting | bytes 16777216 | tf_op jit(solution)/shard_map/all_to_all | solution.py:32
  123.6 12.1 %copy.27 = bf16[128,1,8,4,1024]{4,3,1,0,2:T(4,128)(2,1)} copy(bf16[128,1,8,4,1024]{4,2,3,1,0:T(8,128)(2,1)} %bitcast.50) | data formatting | bytes 16777216 | tf_op jit(solution)/shard_map/all_to_all | solution.py:32
  135.7 6.8 %all-to-all-start.1 = ((bf16[128,1,8,4,1024]{4,3,1,0,2:T(4,128)(2,1)}), bf16[128,1,8,4,1024]{4,3,1,0,2:T(4,128)(2,1)}, u32[]{:S(2)}, u32[]{:S(2)}) async-start(bf16[128,1,8,4,1024]{4,3,1,0,2:T(4,128)(2,1)} %copy.27), calls=%async_computation.1 | async-start | bytes 16777216 | tf_op jit(solution)/shard_map/all_to_all | solution.py:31
  142.5 0.1 constant_dynamic-slice_fusion
  142.6 0.1 copy.24
  142.7 0.1 add_select_fusion
  142.7 0.1 copy.23
  142.8 0.1 select_reduce_fusion
  142.9 182.7 %all-to-all-done.1 = bf16[128,1,8,4,1024]{4,3,1,0,2:T(4,128)(2,1)} async-done(((bf16[128,1,8,4,1024]{4,3,1,0,2:T(4,128)(2,1)}), bf16[128,1,8,4,1024]{4,3,1,0,2:T(4,128)(2,1)}, u32[]{:S(2)}, u32[]{:S(2)}) %all-to-all-start.1) | async-done | bytes 8388640 | tf_op jit(solution)/shard_map/all_to_all | solution.py:31
  325.6 9.4 %copy.28 = bf16[128,1,8,4,1024]{4,0,2,3,1:T(8,128)(2,1)} copy(bf16[128,1,8,4,1024]{4,3,1,0,2:T(4,128)(2,1)} %all-to-all-done.1) | data formatting | bytes 16777216 | tf_op jit(solution)/shard_map/all_to_all | solution.py:31
  335.1 5.8 %fusion.20 = f32[4,1,1024]{2,1,0:T(1,128)S(1)} fusion(bf16[1024,4,1024]{2,0,1:T(8,128)(2,1)} %bitcast.45, bf16[4,1024,1]{1,0,2:T(4,128)(2,1)S(1)} %convert_bitcast_fusion.1), kind=kOutput, calls=%fused_computation.26 | convolution fusion | flops 8388608 | bytes 8413184 | tf_op jit(solution)/shard_map/mbc,bc->bm/dot_general | solution.py:60
  340.9 0.9 collective-permute-start.1
  341.8 0.9 collective-permute-start
  342.6 1.4 collective-permute-done.1
  344.1 0.2 fusion
  344.3 1.2 fusion.18
  345.5 0.6 multiply_reduce_fusion.2
  346.1 41.6 %all-reduce = (f32[]{:T(128)}, f32[]{:T(128)}) all-reduce(f32[]{:T(128)} %get-tuple-element.3, f32[]{:T(128)} %get-tuple-element.2), channel_id=1, replica_groups=mesh['mem'=4,'grid'=8] {'mem','grid'}, use_global_device_ids=true, to_apply=%region_1.2 | all-reduce | flops 2 | bytes 16 | tf_op jit(solution)/shard_map/psum | solution.py:55
  389.0 0.6 multiply_reduce_fusion.1
  389.6 42.7 %psum.30 = f32[]{:T(128)} all-reduce(f32[]{:T(128)} %get-tuple-element.6), channel_id=1, replica_groups=mesh['mem'=4,'grid'=8] {'mem','grid'}, use_global_device_ids=true, to_apply=%region_6.7 | all-reduce | flops 1 | bytes 8 | tf_op jit(solution)/shard_map/psum | solution.py:55
  433.7 5.6 %fusion.16 = f32[4,1,1024]{2,1,0:T(1,128)S(1)} fusion(bf16[1024,4,1024]{2,0,1:T(8,128)(2,1)} %bitcast.46, bf16[4,1024,1]{1,0,2:T(4,128)(2,1)S(1)} %convert_bitcast_fusion), kind=kOutput, calls=%fused_computation.21 | convolution fusion | flops 8388608 | bytes 8413184 | tf_op jit(solution)/shard_map/mbc,bc->bm/dot_general | solution.py:60
  439.3 1.3 collective-permute-start.3
  440.7 0.4 collective-permute-start.2
  441.1 1.4 collective-permute-done.3
  442.5 0.9 collective-permute-done.2
  443.4 0.2 fusion.1
  443.7 4.6 fusion.14
  448.2 0.6 multiply_reduce_fusion
  448.8 41.9 %psum.31 = f32[]{:T(128)} all-reduce(f32[]{:T(128)} %multiply_reduce_fusion), channel_id=1, replica_groups=mesh['mem'=4,'grid'=8] {'mem','grid'}, use_global_device_ids=true, to_apply=%region_8.9 | all-reduce | flops 1 | bytes 8 | tf_op jit(solution)/shard_map/psum | solution.py:67
  492.0 0.6 multiply_subtract_fusion
  (16 shorter events, 0.1 us)
Async XLA Ops:
  0.6 141.9 %copy-start = (f32[128,8]{0,1:T(8,128)S(1)}, f32[128,8]{0,1:T(8,128)}, u32[]{:S(2)}) copy-start(f32[128,8]{0,1:T(8,128)} %param.9) | copy-start | bytes 12292
  135.7 6.9 %copy-start.4 = (s32[128,8]{0,1:T(8,128)S(1)}, s32[128,8]{0,1:T(8,128)}, u32[]{:S(2)}) copy-start(s32[128,8]{0,1:T(8,128)} %param.8) | copy-start | bytes 12292
  135.7 7.2 %copy-start.2 = (f32[4,1024]{1,0:T(4,128)S(1)}, f32[4,1024]{1,0:T(4,128)}, u32[]{:S(2)}) copy-start(f32[4,1024]{1,0:T(4,128)} %param.6) | copy-start | bytes 49156
  135.7 189.9 %all-to-all-start.1 = ((bf16[128,1,8,4,1024]{4,3,1,0,2:T(4,128)(2,1)}), bf16[128,1,8,4,1024]{4,3,1,0,2:T(4,128)(2,1)}, u32[]{:S(2)}, u32[]{:S(2)}) async-start(bf16[128,1,8,4,1024]{4,3,1,0,2:T(4,128)(2,1)} %copy.27), calls=%async_computation.1 | async-start | bytes 16777216 | tf_op jit(solution)/shard_map/all_to_all | solution.py:31
  335.1 9.2 %copy-start.1 = (bf16[128,1,8,4,1024]{4,0,2,3,1:T(8,128)(2,1)S(1)}, bf16[128,1,8,4,1024]{4,0,2,3,1:T(8,128)(2,1)}, u32[]{:S(2)}) copy-start(bf16[128,1,8,4,1024]{4,0,2,3,1:T(8,128)(2,1)} %copy.28) | copy-start | bytes 25165828
  335.1 10.4 %copy-start.3 = (f32[4,1024]{1,0:T(4,128)S(1)}, f32[4,1024]{1,0:T(4,128)}, u32[]{:S(2)}) copy-start(f32[4,1024]{1,0:T(4,128)} %param.7) | copy-start | bytes 49156
  340.9 3.2 collective-permute-start.1
  341.8 2.3 collective-permute-start
  439.3 3.2 collective-permute-start.3
  440.7 2.8 collective-permute-start.2
where the time goes:
time: 496 us; the launch traced here: 493 us
  blocking collectives  226 us (46%)
  waiting for transfers between devices  186 us (38%)
  local copies, waits for them, and re-layouts  44.5 us (9%)
  matrix products  17.7 us (4%)
  starting transfers between devices  10.3 us (2%)
    all_to_all x1, waiting for transfers between devices, per_device(): lax.all_to_all(lax.all_to_all(sectioned, 'mem', split_axis=1, concat_axis...  183 us
    all_to_all x1, blocking collectives, per_device(): lax.all_to_all(sectioned, 'mem', split_axis=1, concat_axis=0, tiled=True)  100 us
    psum x2, blocking collectives, squares(): return lax.psum(jnp.sum(field * field), ('mem', 'grid'))  84.3 us
    psum x1, blocking collectives, per_device(): alpha = norm_now / lax.psum(jnp.sum(direction * image), ('mem', 'grid'))  41.9 us
    all_to_all x2, local copies, waits for them, and re-layouts, per_device(): lax.all_to_all(sectioned, 'mem', split_axis=1, concat_axis=0, tiled=True)  23.5 us
    dot_general x2, matrix products, per_device(): jnp.einsum('mbc,bc->bm', relaid, rounded, preferred_element_type=jnp.floa...  11.4 us
    unnamed x11, local copies, waits for them, and re-layouts  11.3 us
  transfers between devices with their start and end apart: 5, of which 4 were waited for; matrix products, arithmetic and copies ran while one was open for 0% of the time, Pallas kernels for 0%

commit v1 on v0

v1 whole, which is shorter than its diff:
```python
import functools

import jax
import jax.numpy as jnp
from jax import lax
from jax.experimental import pallas as pl
from jax.experimental.pallas import tpu as pltpu
from jax.sharding import PartitionSpec as P

AXES = ("mem", "grid")
M = 1024
LANES = 128
KEEP = 0.25
REACH = 3
F32 = jnp.float32
BF16 = jnp.bfloat16
VMEM = pl.BlockSpec(memory_space=pltpu.VMEM)


def halves_of(x):
    blocks, cells = x.shape
    tiles = cells // (2 * LANES)
    return x.reshape(blocks, 2, tiles, LANES).transpose(1, 0, 2, 3).reshape(2, blocks * tiles, LANES)


def whole_of(x, blocks):
    tiles = x.shape[1] // blocks
    return x.reshape(2, blocks, tiles, LANES).transpose(1, 0, 2, 3).reshape(blocks, 2 * tiles * LANES)


def core_index():
    return lax.rem(lax.axis_index("grid"), 2)


def block_sums(ens_ref, fields, sums_ref, rows, tiles):
    members, blocks, cells = ens_ref.shape
    core = core_index()
    lane = lax.broadcasted_iota(jnp.int32, (rows, LANES), 1)

    def group(g, _):
        base = pl.multiple_of(g * rows, rows)
        parts = []
        for slot in range(2):
            col = lax.rem(core + slot, 2) * (cells // 2)
            for t in range(tiles):
                at = pl.ds(g * rows * tiles + t, rows, stride=tiles)
                parts.append((pl.multiple_of(col + t * LANES, LANES), fields[slot][at, :]))
        out = jnp.zeros((rows, LANES), F32)
        for k in range(members):
            acc = None
            for at, part in parts:
                term = ens_ref[k, pl.ds(base, rows), pl.ds(at, LANES)].astype(F32) * part
                acc = term if acc is None else acc + term
            out = jnp.where(lane == k, jnp.sum(acc, axis=1, keepdims=True), out)
        sums_ref[pl.ds(base, rows), :] = out
        return 0

    lax.fori_loop(0, blocks // rows, group, 0)


def mixed(sums, pad_ref, nbr_ref, weight_ref):
    blocks = sums.shape[0]
    pad_ref[pl.ds(8, blocks), :] = sums
    pad_ref[pl.ds(0, 8), :] = sums[blocks - 8 :]
    pad_ref[pl.ds(8 + blocks, 8), :] = sums[:8]
    away = nbr_ref[...] - lax.broadcasted_iota(jnp.int32, nbr_ref.shape, 0)
    away = jnp.where(away > blocks // 2, away - blocks, away)
    away = jnp.where(away < -(blocks // 2), away + blocks, away)
    total = sums
    for step in range(-REACH, REACH + 1):
        share = jnp.sum(jnp.where(away == step, weight_ref[...], 0.0), axis=1, keepdims=True)
        total = total + share * pad_ref[pl.ds(8 + step, blocks), :]
    return total.astype(BF16).astype(F32)


def spreads(ens_ref, coeff_ref, outs, rows, tiles):
    members, blocks, cells = ens_ref.shape
    core = core_index()

    def group(g, _):
        base = pl.multiple_of(g * rows, rows)
        coeff = coeff_ref[pl.ds(base, rows), :]
        acc = [None] * (2 * tiles)
        for k in range(members):
            one = jnp.broadcast_to(coeff[:, k : k + 1], (rows, LANES))
            for slot in range(2):
                col = lax.rem(core + slot, 2) * (cells // 2)
                for t in range(tiles):
                    at = pl.multiple_of(col + t * LANES, LANES)
                    term = ens_ref[k, pl.ds(base, rows), pl.ds(at, LANES)].astype(F32) * one
                    i = slot * tiles + t
                    acc[i] = term if acc[i] is None else acc[i] + term
        for slot in range(2):
            for t in range(tiles):
                outs[slot][pl.ds(g * rows * tiles + t, rows, stride=tiles), :] = acc[slot * tiles + t]
        return 0

    lax.fori_loop(0, blocks // rows, group, 0)


def by_block(x, blocks):
    tiles = x.shape[0] // blocks
    return jnp.sum(x, axis=1, keepdims=True).reshape(blocks, tiles)


def first_kernel(tiles, ens_ref, mine_ref, other_ref, nbr_ref, weight_ref, own_ref, send_ref, sums_ref, fields, pad_ref, coeff_ref):
    fields[0] = mine_ref[...].astype(F32)
    fields[1] = other_ref[...].astype(F32)
    block_sums(ens_ref, (fields.at[0], fields.at[1]), sums_ref, 16, tiles)
    coeff_ref[...] = mixed(sums_ref[...], pad_ref, nbr_ref, weight_ref)
    spreads(ens_ref, coeff_ref, (own_ref, send_ref), 16, tiles)


def second_kernel(
    tiles, ens_ref, dm_ref, do_ref, pm_ref, po_ref, nbr_ref, weight_ref, sums0_ref, d_own_ref, q_own_ref, obs_ref,
    own_ref, send_ref, scal_ref, fields, sums_ref, pad_ref, coeff_ref,
):
    blocks = ens_ref.shape[1]
    fields[0] = pm_ref[...].astype(F32)
    fields[1] = po_ref[...].astype(F32)
    block_sums(ens_ref, (fields.at[0], fields.at[1]), sums_ref, 16, tiles)
    prod = jnp.zeros((blocks, LANES), F32)
    self = jnp.zeros((blocks, LANES), F32)
    dirs = []
    gots = []
    fields[2] = dm_ref[...].astype(F32)
    fields[3] = do_ref[...].astype(F32)
    for slot in range(2):
        for t in range(tiles):
            d = fields[2 + slot, pl.ds(t, blocks, stride=tiles), :]
            p = fields[slot, pl.ds(t, blocks, stride=tiles), :]
            prod = prod + d * p
            self = self + d * d
    pd = jnp.sum(prod, axis=1, keepdims=True)
    dd = jnp.sum(self, axis=1, keepdims=True)
    tau = jnp.where(dd > 0.0, (1.0 / KEEP - 1.0) * pd / jnp.where(dd > 0.0, dd, 1.0), 0.0)
    rr0 = jnp.sum(dd)
    alpha = rr0 / jnp.sum(pd + tau * dd)
    keep = 1.0 - alpha * tau
    left = jnp.zeros((blocks, LANES), F32)
    for slot in range(2):
        for t in range(tiles):
            d = fields[2 + slot, pl.ds(t, blocks, stride=tiles), :]
            p = fields[slot, pl.ds(t, blocks, stride=tiles), :]
            r = keep * d - alpha * p
            left = left + r * r
    rr1 = jnp.sum(left)
    beta = rr1 / rr0
    sums = (beta + keep) * sums0_ref[...] - alpha * sums_ref[...]
    coeff = mixed(sums, pad_ref, nbr_ref, weight_ref)
    coeff_ref[...] = coeff
    direction = (1.0 + beta) * d_own_ref[...] - alpha * q_own_ref[...]
    part = jnp.sum(sums * coeff) * (1.0 / M) + jnp.sum(obs_ref[...] * direction * direction)
    row = lax.broadcasted_iota(jnp.int32, (8, LANES), 0)
    scal_ref[...] = jnp.where(row == 0, part, jnp.where(row == 1, alpha, jnp.where(row == 2, beta, rr1)))
    spreads(ens_ref, coeff_ref, (own_ref, send_ref), 16, tiles)


def params():
    return pltpu.CompilerParams(vmem_limit_bytes=40 * 1024 * 1024)


def per_device(ensemble, right_side, obs_prec, neighbors, loc_weight):
    own, cells = right_side.shape
    members, blocks, _ = ensemble.shape
    devices = lax.axis_size(AXES)
    tiles = cells // (2 * LANES)
    rows = own * tiles
    pairs = [(i, i ^ 1) for i in range(devices)]
    direct = halves_of(right_side)
    obs = halves_of(obs_prec)

    def gathered(x):
        sent = jnp.broadcast_to(x[None], (devices // 2, 2, rows, LANES)).reshape(devices, rows, LANES)
        mine = lax.all_to_all(sent, AXES, split_axis=0, concat_axis=0, tiled=True).reshape(devices * rows, LANES)
        return mine, lax.ppermute(mine, AXES, pairs)

    def scattered(mine, send):
        both = (mine + lax.ppermute(send, AXES, pairs)).astype(BF16).reshape(devices, rows, LANES)
        return both

    half = jax.ShapeDtypeStruct((blocks * tiles, LANES), F32)
    table = jax.ShapeDtypeStruct((blocks, LANES), F32)
    fields = pltpu.VMEM((2, blocks * tiles, LANES), F32)
    padded = pltpu.VMEM((blocks + 16, LANES), F32)
    coeffs = pltpu.VMEM((blocks, LANES), F32)

    d_mine, d_other = gathered(direct.astype(BF16))
    mine, send, sums0 = pl.pallas_call(
        functools.partial(first_kernel, tiles),
        out_shape=(half, half, table),
        in_specs=[VMEM] * 5,
        out_specs=(VMEM, VMEM, VMEM),
        scratch_shapes=[fields, padded, coeffs],
        compiler_params=params(),
    )(ensemble, d_mine, d_other, neighbors, loc_weight)
    got = lax.all_to_all(scattered(mine, send), AXES, split_axis=0, concat_axis=0, tiled=True)
    spread = jnp.sum(got.reshape(devices // 2, 2, rows, LANES).astype(F32), axis=0)
    q = obs * direct + spread * (1.0 / M)

    d16 = direct.astype(BF16).astype(F32).reshape(2, own, tiles, LANES)
    dd = jnp.sum(d16 * d16, axis=(0, 2, 3), keepdims=True)
    qd = jnp.sum(d16 * q.reshape(d16.shape), axis=(0, 2, 3), keepdims=True)
    tau = jnp.where(dd > 0.0, (1.0 - KEEP) * qd / jnp.where(dd > 0.0, dd, 1.0), 0.0)
    p = (q.reshape(d16.shape) - tau * d16).reshape(q.shape).astype(BF16)
    p_mine, p_other = gathered(p)
    mine, send, scal = pl.pallas_call(
        functools.partial(second_kernel, tiles),
        out_shape=(half, half, jax.ShapeDtypeStruct((8, LANES), F32)),
        in_specs=[VMEM] * 11,
        out_specs=(VMEM, VMEM, VMEM),
        scratch_shapes=[pltpu.VMEM((4, blocks * tiles, LANES), F32), coeffs, padded, coeffs],
        compiler_params=params(),
    )(ensemble, d_mine, d_other, p_mine, p_other, neighbors, loc_weight, sums0, direct, q, obs)
    part, alpha, beta, rr1 = (scal[0, 0], scal[1, 0], scal[2, 0], scal[3, 0])
    high = part.astype(BF16)
    rest = part - high.astype(F32)
    middle = rest.astype(BF16)
    low = (rest - middle.astype(F32)).astype(BF16)
    extra = jnp.broadcast_to(jnp.stack([high, middle, low] + [jnp.zeros_like(low)] * 5)[None, :, None], (devices, 8, LANES))
    sent = jnp.concatenate([scattered(mine, send), extra], axis=1)
    got = lax.all_to_all(sent, AXES, split_axis=0, concat_axis=0, tiled=True).astype(F32)
    spread = jnp.sum(got[:, :rows].reshape(devices // 2, 2, rows, LANES), axis=0)
    denom = jnp.sum(got[:, rows:, 0])
    residual = direct - alpha * q
    direction = residual + beta * direct
    image = obs * direction + spread * (1.0 / M)
    alpha1 = rr1 / denom
    solution_field = alpha * direct + alpha1 * direction
    residual = residual - alpha1 * image
    return whole_of(solution_field, own), whole_of(residual, own)


def solution(mesh):
    return jax.shard_map(
        per_device,
        mesh=mesh,
        in_specs=(
            P(AXES, None, None),
            P(AXES, None),
            P(AXES, None),
            P(),
            P(),
        ),
        out_specs=(P(AXES, None), P(AXES, None)),
        check_vma=False,
    )
```

time: 496 us -> 81.2 us (0.16)
  blocking collectives: 226 us -> 36.1 us
  waiting for transfers between devices: 186 us -> 10.7 us
  local copies, waits for them, and re-layouts: 44.5 us -> 11.2 us
  matrix products: 17.7 us -> 0 us
  Pallas kernels: 0 us -> 12.9 us
  starting transfers between devices: 10.3 us -> 3.51 us
    all_to_all x1, waiting for transfers between devices: 183 us -> 8.33 us  [per_device(): lax.all_to_all(scattered(mine, send), AXES, split_axis=0, concat_axis=0,...]
    psum x3 -> x0, blocking collectives: 126 us -> none  [the longest x2 84.3 us: squares(): return lax.psum(jnp.sum(field * field), ('mem', 'grid'))]
    all_to_all x1 -> x3, blocking collectives: 100 us -> 36.1 us  [the longest x2 25 us: gathered(): lax.all_to_all(sent, AXES, split_axis=0, concat_axis=0, tiled=True)]
    all_to_all x3 -> x0, local copies, waits for them, and re-layouts: 33 us -> none  [the longest x2 23.5 us: per_device(): lax.all_to_all(sectioned, 'mem', split_axis=1, concat_axis=0, tiled=True)]
    dot_general x6 -> x0, matrix products: 17.7 us -> none  [the longest x2 11.4 us: per_device(): jnp.einsum('mbc,bc->bm', relaid, rounded, preferred_element_type=jnp.floa...]
    pallas_call x0 -> x2, Pallas kernels: none -> 12.9 us  [the longest x1 6.75 us: per_device(): pl.pallas_call(functools.partial(second_kernel, tiles), out_shape=(half,...]
    unnamed x11 -> x8, local copies, waits for them, and re-layouts: 11.3 us -> 8.34 us
  transfers between devices with their start and end apart: 5 -> 5, of which waited for: 4 -> 3; matrix products, arithmetic and copies ran while one was open for 0% -> 3% of each run, Pallas kernels for 0% -> 0%
where the time goes in v1:
time: 81.2 us; the launch traced here: 80.8 us
  blocking collectives  36.1 us (44%)
  Pallas kernels  12.9 us (16%)
  local copies, waits for them, and re-layouts  11.2 us (14%)
  waiting for transfers between devices  10.7 us (13%)
  starting transfers between devices  3.51 us (4%)
  between operations  3.31 us (4%)
  other arithmetic  3.08 us (4%)
    all_to_all x2, blocking collectives, gathered(): lax.all_to_all(sent, AXES, split_axis=0, concat_axis=0, tiled=True)  25 us
    all_to_all x1, blocking collectives, per_device(): lax.all_to_all(sent, AXES, split_axis=0, concat_axis=0, tiled=True)  11.1 us
    unnamed x8, local copies, waits for them, and re-layouts  8.34 us
    all_to_all x1, waiting for transfers between devices, per_device(): lax.all_to_all(scattered(mine, send), AXES, split_axis=0, concat_axis=0,...  8.33 us
    pallas_call x1, Pallas kernels, per_device(): pl.pallas_call(functools.partial(second_kernel, tiles), out_shape=(half,...  6.75 us
    pallas_call x1, Pallas kernels, per_device(): pl.pallas_call(functools.partial(first_kernel, tiles), out_shape=(half, h...  6.14 us
    all_to_all x1, starting transfers between devices, per_device(): lax.all_to_all(scattered(mine, send), AXES, split_axis=0, concat_axis=0,...  2.48 us
  transfers between devices with their start and end apart: 5, of which 3 were waited for; matrix products, arithmetic and copies ran while one was open for 3% of the time, Pallas kernels for 0%

profile of v1, /device:TPU:1, one launch (start us, length us, event | category | flops | bytes accessed | tf_op | source)
XLA Modules:
  0.0 80.8 jit_solution(8152301843753746423)
XLA Ops:
  0.6 0.7 reshape.86
  1.4 15.1 %all_to_all.20 = bf16[32,16,128]{2,1,0:T(8,128)(2,1)S(1)} all-to-all(bf16[32,16,128]{2,1,0:T(8,128)(2,1)S(1)} %bitcast.95), channel_id=1, replica_groups=mesh['mem'=4,'grid'=8] {'mem','grid'}, dimensions={0} | all-to-all | bytes 262144 | tf_op jit(solution)/shard_map/all_to_all | solution.py:175
  16.6 0.2 collective-permute-start
  16.8 0.8 copy.10.weight_ref
  17.6 0.8 copy.9.nbr_ref
  18.3 0.0 collective-permute-done.other_ref.do_ref
  18.3 0.0 copy-start
  18.4 3.4 %copy-done = bf16[32,128,1024]{2,1,0:T(8,128)(2,1)S(1)} copy-done((bf16[32,128,1024]{2,1,0:T(8,128)(2,1)S(1)}, bf16[32,128,1024]{2,1,0:T(8,128)(2,1)}, u32[]{:S(2)}) %copy-start) | copy-done | bytes 8388632
  21.7 6.1 %shard_map.68 = (f32[512,128]{1,0:T(8,128)S(1)}, f32[512,128]{1,0:T(8,128)S(1)}, f32[128,128]{1,0:T(8,128)S(1)}) custom-call(bf16[32,128,1024]{2,1,0:T(8,128)(2,1)S(1)} %copy-done, bf16[512,128]{1,0:T(8,128)(2,1)S(1)} %bitcast.83, bf16[512,128]{1,0:T(8,128)(2,1)S(1)} %collective-permute-done.other_ref.do_ref, s32[128,8]{1,0:T(8,128)S(1)} %copy.9.nbr_ref, ...), custom_call_target="tpu_custom_call" | custom-call | tf_op jit(solution)/shard_map/pallas_call | solution.py:189
  27.9 0.4 collective-permute-start.1
  28.3 1.2 %collective-permute-done.1 = f32[512,128]{1,0:T(8,128)S(1)} collective-permute-done((f32[512,128]{1,0:T(8,128)S(1)}, f32[512,128]{1,0:T(8,128)S(1)}, u32[]{:S(2)}, u32[]{:S(2)}) %collective-permute-start.1) | collective-permute-done | bytes 262176 | tf_op jit(solution)/shard_map/ppermute | solution.py:179
  29.5 0.7 add_convert_fusion.1
  30.2 2.5 %all-to-all-start.1 = ((bf16[32,16,128]{2,1,0:T(8,128)(2,1)}), bf16[32,16,128]{2,1,0:T(8,128)(2,1)S(1)}, u32[]{:S(2)}, u32[]{:S(2)}) async-start(bf16[32,16,128]{2,1,0:T(8,128)(2,1)} %bitcast.5), calls=%async_computation.1 | async-start | bytes 262144 | tf_op jit(solution)/shard_map/all_to_all | solution.py:197
  32.7 8.3 %all-to-all-done.1 = bf16[32,16,128]{2,1,0:T(8,128)(2,1)S(1)} async-done(((bf16[32,16,128]{2,1,0:T(8,128)(2,1)}), bf16[32,16,128]{2,1,0:T(8,128)(2,1)S(1)}, u32[]{:S(2)}, u32[]{:S(2)}) %all-to-all-start.1) | async-done | bytes 131104 | tf_op jit(solution)/shard_map/all_to_all | solution.py:197
  41.1 0.1 fusion.1
  41.2 0.1 fusion.3
  41.3 9.9 %all_to_all.21 = bf16[32,16,128]{2,1,0:T(8,128)(2,1)S(1)} all-to-all(bf16[32,16,128]{2,1,0:T(8,128)(2,1)S(1)} %bitcast.96), channel_id=1, replica_groups=mesh['mem'=4,'grid'=8] {'mem','grid'}, dimensions={0} | all-to-all | bytes 262144 | tf_op jit(solution)/shard_map/all_to_all | solution.py:175
  51.2 0.2 collective-permute-start.2
  51.4 1.2 %collective-permute-done.2.po_ref = bf16[512,128]{1,0:T(8,128)(2,1)S(1)} collective-permute-done((bf16[512,128]{1,0:T(8,128)(2,1)S(1)}, bf16[512,128]{1,0:T(8,128)(2,1)S(1)}, u32[]{:S(2)}, u32[]{:S(2)}) %collective-permute-start.2) | collective-permute-done | bytes 131104 | tf_op jit(solution)/shard_map/ppermute | solution.py:176
  52.5 3.4 %copy-done.1 = bf16[32,128,1024]{2,1,0:T(8,128)(2,1)S(1)} copy-done((bf16[32,128,1024]{2,1,0:T(8,128)(2,1)S(1)}, bf16[32,128,1024]{2,1,0:T(8,128)(2,1)}, u32[]{:S(2)}) %copy-start.1) | copy-done | bytes 8388632
  55.9 6.7 %shard_map.69 = (f32[512,128]{1,0:T(8,128)S(1)}, f32[512,128]{1,0:T(8,128)S(1)}, f32[8,128]{1,0:T(8,128)S(1)}) custom-call(bf16[32,128,1024]{2,1,0:T(8,128)(2,1)S(1)} %copy-done.1, bf16[512,128]{1,0:T(8,128)(2,1)S(1)} %bitcast.84, bf16[512,128]{1,0:T(8,128)(2,1)S(1)} %collective-permute-done.other_ref.do_ref, bf16[512,128]{1,0:T(8,128)(2,1)S(1)} %bitcast.86, ...), custom_call_target="tpu_custom_call" | custom-call | tf_op jit(solution)/shard_map/pallas_call | solution.py:207
  62.7 0.3 collective-permute-start.3
  62.9 0.6 fusion.13
  64.8 0.1 stack.15
  64.9 0.1 pad.1.clone
  65.0 0.0 collective-permute-done.3
  65.0 0.1 pad_maximum_fusion
  65.1 11.1 %all_to_all.22 = bf16[32,24,128]{2,1,0:T(8,128)(2,1)S(1)} all-to-all(bf16[32,24,128]{2,1,0:T(8,128)(2,1)S(1)} %pad_maximum_fusion), channel_id=1, replica_groups=mesh['mem'=4,'grid'=8] {'mem','grid'}, dimensions={0} | all-to-all | bytes 393216 | tf_op jit(solution)/shard_map/all_to_all | solution.py:222
  76.2 0.7 slice_reduce_fusion
  78.2 1.3 %fusion.8 = (f32[4,2,4,128]{3,2,0,1:T(4,128)S(1)}, f32[4,2,4,128]{3,2,0,1:T(4,128)S(1)}) fusion(f32[2,4,4,128]{3,2,1,0:T(4,128)S(1)} %bitcast.100, f32[]{:T(128)} %bitcast.20, f32[]{:T(128)S(6)} %div.12, f32[]{:T(128)} %bitcast.13, f32[4,2,4,128]{3,2,1,0:T(4,128)S(1)} %reshape.90, f32[2,4,4,128]{3,2,1,0:T(4,128)S(1)} %bitcast.99, ...), kind=kLoop, calls=%fused_computation.18 | loop fusion | flops 53248 | bytes 98316 | tf_op jit(solution)/shard_map/transpose | solution.py:28
  79.5 0.6 reshape.96
  80.1 0.6 reshape.98
  (20 shorter events, 0.2 us)
Async XLA Ops:
  0.6 32.0 %copy-start.2 = (f32[4,1024]{1,0:T(4,128)S(1)}, f32[4,1024]{1,0:T(4,128)}, u32[]{:S(2)}) copy-start(f32[4,1024]{1,0:T(4,128)} %param.7) | copy-start | bytes 49156
  16.6 1.8 %collective-permute-start = (bf16[512,128]{1,0:T(8,128)(2,1)S(1)}, bf16[512,128]{1,0:T(8,128)(2,1)S(1)}, u32[]{:S(2)}, u32[]{:S(2)}) collective-permute-start(bf16[512,128]{1,0:T(8,128)(2,1)S(1)} %bitcast.82), channel_id=1, source_target_pairs={{0,1},{1,0},{2,3},{3,2},{4,5},{5,4},{6,7},{7,6},{8,9},{9,8},{10,11... | collective-permute-start | bytes 393224 | tf_op jit(solution)/shard_map/ppermute | solution.py:176
  18.3 3.4 %copy-start = (bf16[32,128,1024]{2,1,0:T(8,128)(2,1)S(1)}, bf16[32,128,1024]{2,1,0:T(8,128)(2,1)}, u32[]{:S(2)}) copy-start(bf16[32,128,1024]{2,1,0:T(8,128)(2,1)} %ens_ref.3) | copy-start | bytes 25165828
  27.9 1.6 %collective-permute-start.1 = (f32[512,128]{1,0:T(8,128)S(1)}, f32[512,128]{1,0:T(8,128)S(1)}, u32[]{:S(2)}, u32[]{:S(2)}) collective-permute-start(f32[512,128]{1,0:T(8,128)S(1)} %get-tuple-element.9), channel_id=1, source_target_pairs={{0,1},{1,0},{2,3},{3,2},{4,5},{5,4},{6,7},{7,6},{8,9},{9,8},{10,11... | collective-permute-start | bytes 786440 | tf_op jit(solution)/shard_map/ppermute | solution.py:179
  30.2 10.9 %all-to-all-start.1 = ((bf16[32,16,128]{2,1,0:T(8,128)(2,1)}), bf16[32,16,128]{2,1,0:T(8,128)(2,1)S(1)}, u32[]{:S(2)}, u32[]{:S(2)}) async-start(bf16[32,16,128]{2,1,0:T(8,128)(2,1)} %bitcast.5), calls=%async_computation.1 | async-start | bytes 262144 | tf_op jit(solution)/shard_map/all_to_all | solution.py:197
  51.2 1.3 %collective-permute-start.2 = (bf16[512,128]{1,0:T(8,128)(2,1)S(1)}, bf16[512,128]{1,0:T(8,128)(2,1)S(1)}, u32[]{:S(2)}, u32[]{:S(2)}) collective-permute-start(bf16[512,128]{1,0:T(8,128)(2,1)S(1)} %bitcast.85), channel_id=1, source_target_pairs={{0,1},{1,0},{2,3},{3,2},{4,5},{5,4},{6,7},{7,6},{8,9},{9,8},{10,11... | collective-permute-start | bytes 393224 | tf_op jit(solution)/shard_map/ppermute | solution.py:176
  52.5 3.4 %copy-start.1 = (bf16[32,128,1024]{2,1,0:T(8,128)(2,1)S(1)}, bf16[32,128,1024]{2,1,0:T(8,128)(2,1)}, u32[]{:S(2)}) copy-start(bf16[32,128,1024]{2,1,0:T(8,128)(2,1)} %ens_ref.3) | copy-start | bytes 25165828
  62.7 2.3 %collective-permute-start.3 = (f32[512,128]{1,0:T(8,128)S(1)}, f32[512,128]{1,0:T(8,128)S(1)}, u32[]{:S(2)}, u32[]{:S(2)}) collective-permute-start(f32[512,128]{1,0:T(8,128)S(1)} %get-tuple-element.13), channel_id=1, source_target_pairs={{0,1},{1,0},{2,3},{3,2},{4,5},{5,4},{6,7},{7,6},{8,9},{9,8},{10,11... | collective-permute-start | bytes 786440 | tf_op jit(solution)/shard_map/ppermute | solution.py:179

commit v2 on v0

v2 whole, which is shorter than its diff:
```python
import functools

import jax
import jax.numpy as jnp
from jax import lax
from jax.experimental import pallas as pl
from jax.experimental.pallas import tpu as pltpu
from jax.sharding import PartitionSpec as P

AXES = ("mem", "grid")
M = 1024
LANES = 128
ROWS = 16
KEEP = 0.25
REACH = 3
SHIFTS = range(-REACH, REACH + 1)
F32 = jnp.float32
BF16 = jnp.bfloat16
VMEM = pl.BlockSpec(memory_space=pltpu.VMEM)
HBM = pl.BlockSpec(memory_space=pltpu.HBM)


def core_index():
    return lax.rem(lax.axis_index("grid"), 2)


def every(ref, t, first, blocks, tiles):
    return ref[pl.ds(first * tiles + t, blocks, stride=tiles), :]


def lay_kernel(tiles, field_ref, halves_ref):
    own = field_ref.shape[0]
    for h in range(2):
        for t in range(tiles):
            cells = pl.ds((h * tiles + t) * LANES, LANES)
            halves_ref[pl.ds(h * own * tiles + t, own, stride=tiles), :] = field_ref[:, cells]


def start_kernel(tiles, right_ref, sent_ref, direct_ref):
    lay_kernel(tiles, right_ref, direct_ref)
    spread_out(direct_ref[...].astype(BF16), sent_ref)


def spread_out(both, sent_ref):
    devices, rows, _ = sent_ref.shape
    low, high = both[:rows], both[rows:]
    for chip in range(devices // 2):
        sent_ref[2 * chip] = low
        sent_ref[2 * chip + 1] = high


def load_kernel(
    tiles, ens_hbm, nbr_hbm, weight_hbm, obs_hbm, mine_ref, ens_ref, share_ref, acc_ref, obs_ref,
    held, mine, nbr_ref, weight_ref, laid, sems, small,
):
    members, blocks, cells = ens_hbm.shape
    half = cells // 2
    core = core_index()
    groups = blocks // ROWS

    def copies(g):
        span = pl.ds(pl.multiple_of(g * ROWS, ROWS), ROWS)
        out = []
        for slot in range(2):
            col = pl.multiple_of(lax.rem(core + slot, 2) * half, half)
            source = ens_hbm.at[:, span, pl.ds(col, half)]
            out.append(pltpu.make_async_copy(source, held.at[slot, :, span], sems.at[slot, g]))
        return out

    lists = (
        pltpu.make_async_copy(nbr_hbm, nbr_ref, small.at[0]),
        pltpu.make_async_copy(weight_hbm, weight_ref, small.at[1]),
        pltpu.make_async_copy(obs_hbm, laid, small.at[2]),
    )
    for copy in lists:
        copy.start()

    def begin(g, _):
        for copy in copies(g):
            copy.start()
        return 0

    lax.fori_loop(0, groups, begin, 0)
    mine[...] = mine_ref[...].astype(F32)
    for copy in lists:
        copy.wait()
    lay_kernel(tiles, laid, obs_ref)
    away = nbr_ref[...] - lax.broadcasted_iota(jnp.int32, nbr_ref.shape, 1)
    away = jnp.where(away > blocks // 2, away - blocks, away)
    away = jnp.where(away < -(blocks // 2), away + blocks, away)
    row = lax.broadcasted_iota(jnp.int32, (8, blocks), 0)
    shares = jnp.zeros((8, blocks), F32)
    for i, shift in enumerate(SHIFTS):
        share = jnp.sum(jnp.where(away == shift, weight_ref[...], 0.0), axis=0, keepdims=True)
        shares = jnp.where(row == i, share, shares)
    shares = shares.T
    for i in range(len(SHIFTS)):
        share_ref[i] = jnp.broadcast_to(shares[:, i : i + 1], (blocks, LANES))

    def group(g, _):
        first = pl.multiple_of(g * ROWS, ROWS)
        for copy in copies(g):
            copy.wait()
        parts = [every(mine, t, first, ROWS, tiles) for t in range(tiles)]
        for k in range(members):
            acc = None
            for t in range(tiles):
                cells = pl.ds(t * LANES, LANES)
                one = held[0, k, pl.ds(first, ROWS), cells].astype(F32)
                ens_ref[0, k, pl.ds(first, ROWS), cells] = one
                acc = one * parts[t] if acc is None else acc + one * parts[t]
            acc_ref[k, pl.ds(first, ROWS), :] = acc
            for t in range(tiles):
                cells = pl.ds(t * LANES, LANES)
                ens_ref[1, k, pl.ds(first, ROWS), cells] = held[1, k, pl.ds(first, ROWS), cells].astype(F32)
        return 0

    lax.fori_loop(0, groups, group, 0)


def own_sums_kernel(tiles, ens_ref, mine_ref, acc_ref, mine):
    _, members, blocks, _ = ens_ref.shape
    mine[...] = mine_ref[...].astype(F32)

    def group(g, _):
        first = pl.multiple_of(g * ROWS, ROWS)
        parts = [every(mine, t, first, ROWS, tiles) for t in range(tiles)]
        for k in range(members):
            acc = None
            for t in range(tiles):
                term = ens_ref[0, k, pl.ds(first, ROWS), pl.ds(t * LANES, LANES)] * parts[t]
                acc = term if acc is None else acc + term
            acc_ref[k, pl.ds(first, ROWS), :] = acc
        return 0

    lax.fori_loop(0, blocks // ROWS, group, 0)


def block_sums(ens_ref, acc_ref, field, sums_ref, tiles):
    _, members, blocks, _ = ens_ref.shape
    lane = lax.broadcasted_iota(jnp.int32, (ROWS, LANES), 1)

    def group(g, _):
        first = pl.multiple_of(g * ROWS, ROWS)
        parts = [every(field, t, first, ROWS, tiles) for t in range(tiles)]
        out = jnp.zeros((ROWS, LANES), F32)
        for k in range(members):
            acc = acc_ref[k, pl.ds(first, ROWS), :]
            for t in range(tiles):
                acc = acc + ens_ref[1, k, pl.ds(first, ROWS), pl.ds(t * LANES, LANES)] * parts[t]
            out = jnp.where(lane == k, jnp.sum(acc, axis=1, keepdims=True), out)
        sums_ref[pl.ds(first, ROWS), :] = out
        return 0

    lax.fori_loop(0, blocks // ROWS, group, 0)


def mixed(sums, pad_ref, share_ref):
    blocks = sums.shape[0]
    pad_ref[pl.ds(8, blocks), :] = sums
    pad_ref[pl.ds(0, 8), :] = sums[blocks - 8 :]
    pad_ref[pl.ds(8 + blocks, 8), :] = sums[:8]
    total = sums
    for i, shift in enumerate(SHIFTS):
        total = total + share_ref[i] * pad_ref[pl.ds(8 + shift, blocks), :]
    return total.astype(BF16).astype(F32)


def half_spread(ens_ref, slot, coeff, wide_ref, out_ref, tiles):
    _, members, blocks, _ = ens_ref.shape

    def group(g, _):
        first = pl.multiple_of(g * ROWS, ROWS)
        here = None if coeff is None else coeff[pl.ds(first, ROWS), :]
        acc = [None] * tiles
        for k in range(members):
            if here is None:
                one = wide_ref[k, pl.ds(first, ROWS), :]
            else:
                one = jnp.broadcast_to(here[:, k : k + 1], (ROWS, LANES))
                wide_ref[k, pl.ds(first, ROWS), :] = one
            for t in range(tiles):
                term = ens_ref[slot, k, pl.ds(first, ROWS), pl.ds(t * LANES, LANES)] * one
                acc[t] = term if acc[t] is None else acc[t] + term
        for t in range(tiles):
            out_ref[pl.ds(first * tiles + t, ROWS, stride=tiles), :] = acc[t]
        return 0

    lax.fori_loop(0, blocks // ROWS, group, 0)


def first_kernel(tiles, ens_ref, acc_ref, other_ref, share_ref, send_ref, sums_ref, wide_ref, other, pad_ref, coeff_ref):
    other[...] = other_ref[...].astype(F32)
    block_sums(ens_ref, acc_ref, other, sums_ref, tiles)
    coeff_ref[...] = mixed(sums_ref[...], pad_ref, share_ref)
    half_spread(ens_ref, 1, coeff_ref, wide_ref, send_ref, tiles)


def own_kernel(tiles, ens_ref, wide_ref, own_ref):
    half_spread(ens_ref, 0, None, wide_ref, own_ref, tiles)


def received(got, rows):
    devices = got.shape[0]
    sums = []
    for core in range(2):
        total = None
        for chip in range(devices // 2):
            one = got[2 * chip + core, :rows, :].astype(F32)
            total = one if total is None else total + one
        sums.append(total)
    return jnp.concatenate(sums, axis=0)


def middle_kernel(tiles, got_ref, direct_ref, obs_ref, q_ref, sent_ref):
    _, rows, _ = got_ref.shape
    direct = direct_ref[...]
    q = obs_ref[...] * direct + received(got_ref, rows) * (1.0 / M)
    q_ref[...] = q
    d = direct.astype(BF16).astype(F32)
    dd = jnp.sum(d * d, axis=1, keepdims=True)
    qd = jnp.sum(d * q, axis=1, keepdims=True)
    row = lax.broadcasted_iota(jnp.int32, dd.shape, 0) % rows // tiles
    tau = jnp.zeros_like(dd)
    for b in range(rows // tiles):
        here = row == b
        self = jnp.sum(jnp.where(here, dd, 0.0), axis=0, keepdims=True)
        prod = jnp.sum(jnp.where(here, qd, 0.0), axis=0, keepdims=True)
        share = jnp.where(self > 0.0, (1.0 - KEEP) * prod / jnp.where(self > 0.0, self, 1.0), 0.0)
        tau = jnp.where(here, share, tau)
    spread_out((q - tau * d).astype(BF16), sent_ref)


def second_kernel(
    tiles, ens_ref, acc_ref, dm_ref, do_ref, pm_ref, po_ref, share_ref, sums0_ref, direct_ref, q_ref, obs_ref,
    send_ref, wide_ref, scal_ref, extra_ref, mine, other, dm, do, sums_ref, pad_ref, coeff_ref,
):
    blocks = ens_ref.shape[2]
    mine[...] = pm_ref[...].astype(F32)
    other[...] = po_ref[...].astype(F32)
    dm[...] = dm_ref[...].astype(F32)
    do[...] = do_ref[...].astype(F32)
    block_sums(ens_ref, acc_ref, other, sums_ref, tiles)
    prod = jnp.zeros((blocks, LANES), F32)
    self = jnp.zeros((blocks, LANES), F32)
    halves = ((dm, mine), (do, other))
    for d_ref, p_ref in halves:
        for t in range(tiles):
            d = every(d_ref, t, 0, blocks, tiles)
            prod = prod + d * every(p_ref, t, 0, blocks, tiles)
            self = self + d * d
    pd = jnp.sum(prod, axis=1, keepdims=True)
    dd = jnp.sum(self, axis=1, keepdims=True)
    tau = jnp.where(dd > 0.0, (1.0 / KEEP - 1.0) * pd / jnp.where(dd > 0.0, dd, 1.0), 0.0)
    rr0 = jnp.sum(dd, axis=0, keepdims=True)
    alpha = rr0 / jnp.sum(pd + tau * dd, axis=0, keepdims=True)
    keep = 1.0 - alpha * tau
    left = jnp.zeros((blocks, LANES), F32)
    for d_ref, p_ref in halves:
        for t in range(tiles):
            r = keep * every(d_ref, t, 0, blocks, tiles) - alpha * every(p_ref, t, 0, blocks, tiles)
            left = left + r * r
    rr1 = jnp.sum(jnp.sum(left, axis=1, keepdims=True), axis=0, keepdims=True)
    beta = rr1 / rr0
    sums = (beta + keep) * sums0_ref[...] - alpha * sums_ref[...]
    coeff = mixed(sums, pad_ref, share_ref)
    coeff_ref[...] = coeff
    direction = (1.0 + beta) * direct_ref[...] - alpha * q_ref[...]
    part = jnp.sum(jnp.sum(sums * coeff, axis=0, keepdims=True), axis=1, keepdims=True) * (1.0 / M)
    part += jnp.sum(jnp.sum(obs_ref[...] * direction * direction, axis=0, keepdims=True), axis=1, keepdims=True)
    row = lax.broadcasted_iota(jnp.int32, (8, LANES), 0)
    scal_ref[...] = jnp.where(row == 0, alpha, jnp.where(row == 1, beta, rr1))
    high = part.astype(BF16).astype(F32)
    mid = (part - high).astype(BF16).astype(F32)
    extra_ref[...] = jnp.where(row == 0, high, jnp.where(row == 1, mid, jnp.where(row == 2, part - high - mid, 0.0)))
    half_spread(ens_ref, 1, coeff_ref, wide_ref, send_ref, tiles)


def last_kernel(tiles, got_ref, scal_ref, direct_ref, obs_ref, q_ref, solution_ref, residual_ref, sol, res):
    devices, rows, _ = got_ref.shape
    rows -= 8
    denom = jnp.zeros((8, LANES), F32)
    for i in range(devices):
        denom = denom + got_ref[i, rows:, :].astype(F32)
    denom = jnp.sum(denom, axis=0, keepdims=True)
    alpha, beta, rr1 = scal_ref[0:1, :], scal_ref[1:2, :], scal_ref[2:3, :]
    direct = direct_ref[...]
    residual = direct - alpha * q_ref[...]
    direction = residual + beta * direct
    image = obs_ref[...] * direction + received(got_ref, rows) * (1.0 / M)
    alpha1 = rr1 / denom
    sol[...] = alpha * direct + alpha1 * direction
    res[...] = residual - alpha1 * image
    own = solution_ref.shape[0]
    for h in range(2):
        for t in range(tiles):
            cells = pl.ds((h * tiles + t) * LANES, LANES)
            at = pl.ds(h * rows + t, own, stride=tiles)
            solution_ref[:, cells] = sol[at, :]
            residual_ref[:, cells] = res[at, :]


def call(kernel, name, outs, ins, scratch=(), mib=8, cost=(0, 0)):
    return pl.pallas_call(
        kernel,
        name=name,
        out_shape=tuple(outs),
        in_specs=ins,
        out_specs=(VMEM,) * len(outs),
        scratch_shapes=list(scratch),
        compiler_params=pltpu.CompilerParams(vmem_limit_bytes=mib * 1024 * 1024),
        cost_estimate=pl.CostEstimate(flops=cost[0], bytes_accessed=cost[1], transcendentals=0),
    )


def per_device(ensemble, right_side, obs_prec, neighbors, loc_weight):
    own, cells = right_side.shape
    members, blocks, _ = ensemble.shape
    devices = lax.axis_size(AXES)
    tiles = cells // (2 * LANES)
    rows = own * tiles
    half = blocks * tiles
    pairs = [(i, i ^ 1) for i in range(devices)]
    shape = jax.ShapeDtypeStruct
    part = functools.partial
    mib = 4 + 4 * blocks // 128

    def swap(x):
        return lax.ppermute(x, AXES, pairs)

    def exchange(x):
        return lax.all_to_all(x, AXES, split_axis=0, concat_axis=0, tiled=True)

    to_all = shape((devices, rows, LANES), BF16)
    lanes = shape((members, blocks, LANES), F32)
    table = shape((blocks, LANES), F32)
    part_half = shape((half, LANES), F32)
    mine = shape((2 * rows, LANES), F32)
    field = pltpu.VMEM((half, LANES), F32)
    padded = pltpu.VMEM((blocks + 16, LANES), F32)
    work = 2 * members * blocks * cells

    sent, direct = call(part(start_kernel, tiles), "start", (to_all, mine), [VMEM])(right_side)
    d_mine = exchange(sent).reshape(half, LANES)
    d_other = swap(d_mine)
    ens, share, acc, obs = call(
        part(load_kernel, tiles),
        "load",
        (shape((2, members, blocks, cells // 2), F32), shape((len(SHIFTS), blocks, LANES), F32), lanes, mine),
        [HBM, HBM, HBM, HBM, VMEM],
        [
            pltpu.VMEM((2, members, blocks, cells // 2), BF16),
            field,
            pltpu.VMEM(neighbors.shape[::-1], jnp.int32),
            pltpu.VMEM(loc_weight.shape[::-1], F32),
            pltpu.VMEM((own, cells), F32),
            pltpu.SemaphoreType.DMA((2, blocks // ROWS)),
            pltpu.SemaphoreType.DMA((3,)),
        ],
        mib=8 + mib,
        cost=(work, 6 * members * blocks * cells),
    )(*(pltpu.with_memory_space_constraint(x, pltpu.HBM) for x in (ensemble, neighbors.T, loc_weight.T, obs_prec)), d_mine)

    coeffs = pltpu.VMEM((blocks, LANES), F32)
    send, sums0, wide = call(
        part(first_kernel, tiles), "first", (part_half, table, lanes), [VMEM] * 4, [field, padded, coeffs],
        mib=mib, cost=(work, 0),
    )(ens, acc, d_other, share)
    (kept,) = call(part(own_kernel, tiles), "own", (part_half,), [VMEM] * 2, mib=mib, cost=(work, 0))(ens, wide)
    got = exchange((kept + swap(send)).astype(BF16).reshape(to_all.shape))

    q, sent = call(part(middle_kernel, tiles), "middle", (mine, to_all), [VMEM] * 3)(got, direct, obs)
    p_mine = exchange(sent).reshape(half, LANES)
    p_other = swap(p_mine)

    small = shape((8, LANES), F32)
    (acc,) = call(part(own_sums_kernel, tiles), "sums", (lanes,), [VMEM] * 2, [field], mib=mib, cost=(work, 0))(ens, p_mine)
    send, wide, scal, extra = call(
        part(second_kernel, tiles),
        "second",
        (part_half, lanes, small, small),
        [VMEM] * 11,
        [field] * 4 + [coeffs, padded, coeffs],
        mib=mib, cost=(work, 0),
    )(ens, acc, d_mine, d_other, p_mine, p_other, share, sums0, direct, q, obs)
    (kept,) = call(part(own_kernel, tiles), "own", (part_half,), [VMEM] * 2, mib=mib, cost=(work, 0))(ens, wide)
    both = (kept + swap(send)).reshape(to_all.shape)
    both = jnp.concatenate([both, jnp.broadcast_to(extra[None], (devices, 8, LANES))], axis=1)
    got = exchange(both.astype(BF16))
    out = shape((own, cells), F32)
    scratch = pltpu.VMEM((2 * rows, LANES), F32)
    return call(part(last_kernel, tiles), "last", (out, out), [VMEM] * 5, [scratch] * 2)(got, scal, direct, obs, q)


def solution(mesh):
    return jax.shard_map(
        per_device,
        mesh=mesh,
        in_specs=(
            P(AXES, None, None),
            P(AXES, None),
            P(AXES, None),
            P(),
            P(),
        ),
        out_specs=(P(AXES, None), P(AXES, None)),
        check_vma=False,
    )
```

time: 496 us -> 63.2 us (0.13)
  waiting for transfers between devices: 186 us -> 1 us
  blocking collectives: 226 us -> 46 us
  local copies, waits for them, and re-layouts: 44.5 us -> 0.72 us
  matrix products: 17.7 us -> 0 us
  Pallas kernels: 0 us -> 13.4 us
  starting transfers between devices: 10.3 us -> 1.03 us
    all_to_all x1 -> x0, waiting for transfers between devices: 183 us -> none  [per_device(): lax.all_to_all(lax.all_to_all(sectioned, 'mem', split_axis=1, concat_axis...]
    psum x3 -> x0, blocking collectives: 126 us -> none  [the longest x2 84.3 us: squares(): return lax.psum(jnp.sum(field * field), ('mem', 'grid'))]
    all_to_all x1 -> x4, blocking collectives: 100 us -> 46 us  [exchange(): return lax.all_to_all(x, AXES, split_axis=0, concat_axis=0, tiled=True)]
    all_to_all x3 -> x0, local copies, waits for them, and re-layouts: 33 us -> none  [the longest x2 23.5 us: per_device(): lax.all_to_all(sectioned, 'mem', split_axis=1, concat_axis=0, tiled=True)]
    dot_general x6 -> x0, matrix products: 17.7 us -> none  [the longest x2 11.4 us: per_device(): jnp.einsum('mbc,bc->bm', relaid, rounded, preferred_element_type=jnp.floa...]
    pallas_call x0 -> x9, Pallas kernels: none -> 13.4 us  [the longest x1 3.81 us: per_device(): call(part(load_kernel, tiles), 'load', (shape((2, members, blocks, cells...]
    unnamed x11 -> x2, local copies, waits for them, and re-layouts: 11.3 us -> 0.71 us
    all_to_all x1 -> x0, starting transfers between devices: 6.78 us -> none  [per_device(): lax.all_to_all(lax.all_to_all(sectioned, 'mem', split_axis=1, concat_axis...]
  transfers between devices with their start and end apart: 5 -> 4, of which waited for: 4 -> 3; matrix products, arithmetic and copies ran while one was open for 0% -> 0% of each run, Pallas kernels for 0% -> 10%
where the time goes in v2:
time: 63.2 us; the launch traced here: 62.9 us
  blocking collectives  46 us (73%)
  Pallas kernels  13.4 us (21%)
  starting transfers between devices  1.03 us (2%)
  waiting for transfers between devices  1 us (2%)
  local copies, waits for them, and re-layouts  0.72 us (1%)
  between operations  0.72 us (1%)
    all_to_all x4, blocking collectives, exchange(): return lax.all_to_all(x, AXES, split_axis=0, concat_axis=0, tiled=True)  46 us
    pallas_call x1, Pallas kernels, per_device(): call(part(load_kernel, tiles), 'load', (shape((2, members, blocks, cells...  3.81 us
    pallas_call x1, Pallas kernels, per_device(): call(part(second_kernel, tiles), 'second', (part_half, lanes, small, smal...  3.28 us
    pallas_call x1, Pallas kernels, per_device(): call(part(first_kernel, tiles), 'first', (part_half, table, lanes), [VMEM...  2.78 us
    pallas_call x2, Pallas kernels, per_device(): call(part(own_kernel, tiles), 'own', (part_half,), [VMEM] * 2, mib=mib, c...  2.15 us
  transfers between devices with their start and end apart: 4, of which 3 were waited for; matrix products, arithmetic and copies ran while one was open for 0% of the time, Pallas kernels for 10%

profile of v2, /device:TPU:1, one launch (start us, length us, event | category | flops | bytes accessed | tf_op | source)
XLA Modules:
  0.0 62.9 jit_solution(17544117924432615314)
XLA Ops:
  0.6 0.0 copy-start
  0.6 0.7 %copy-done = f32[4,1024]{1,0:T(4,128)S(1)} copy-done((f32[4,1024]{1,0:T(4,128)S(1)}, f32[4,1024]{1,0:T(4,128)}, u32[]{:S(2)}) %copy-start) | copy-done | bytes 16408
  1.4 15.1 %all_to_all.20 = bf16[32,16,128]{2,1,0:T(8,128)(2,1)S(1)} all-to-all(bf16[32,16,128]{2,1,0:T(8,128)(2,1)S(1)} %get-tuple-element.17), channel_id=1, replica_groups=mesh['mem'=4,'grid'=8] {'mem','grid'}, dimensions={0} | all-to-all | bytes 262144 | tf_op jit(solution)/shard_map/all_to_all | solution.py:332
  16.5 0.2 collective-permute-start
  16.7 3.8 %load.1 = (f32[2,32,128,512]{3,2,1,0:T(8,128)S(1)}, f32[7,128,128]{2,1,0:T(8,128)S(1)}, f32[32,128,128]{2,1,0:T(8,128)S(1)}, f32[32,128]{1,0:T(8,128)S(1)}) custom-call(bf16[32,128,1024]{2,1,0:T(8,128)(2,1)} %ens_hbm.1, s32[8,128]{1,0:T(8,128)} %bitcast.14, f32[8,128]{1,0:T(8,128)} %bitcast.15, f32[4,1024]{1,0:T(4,128)} %obs_hbm.1, bf16[512,128]{1,0:T(8,128)(2,1)S(1)} %bitcast.7), custom_call_target="tpu_custom_call" | custom-call | flops 8388608 | bytes 25165824 | tf_op jit(solution)/shard_map/load/pallas_call | solution.py:346
  20.5 0.0 collective-permute-done.other_ref.do_ref
  20.5 2.8 %first.1 = (f32[512,128]{1,0:T(8,128)S(1)}, f32[128,128]{1,0:T(8,128)S(1)}, f32[32,128,128]{2,1,0:T(8,128)S(1)}) custom-call(f32[2,32,128,512]{3,2,1,0:T(8,128)S(1)} %get-tuple-element.18.ens_ref, f32[32,128,128]{2,1,0:T(8,128)S(1)} %get-tuple-element.19.acc_ref, bf16[512,128]{1,0:T(8,128)(2,1)S(1)} %collective-permute-done.other_ref.do_ref, ...), custom_call_target="tpu_custom_call" | custom-call | flops 8388608 | tf_op jit(solution)/shard_map/first/pallas_call | solution.py:365
  23.3 0.4 collective-permute-start.1
  23.7 1.1 %own.2 = f32[512,128]{1,0:T(8,128)S(1)} custom-call(f32[2,32,128,512]{3,2,1,0:T(8,128)S(1)} %get-tuple-element.18.ens_ref, f32[32,128,128]{2,1,0:T(8,128)S(1)} %get-tuple-element.21.wide_ref), custom_call_target="tpu_custom_call" | custom-call | flops 8388608 | tf_op jit(solution)/shard_map/own/pallas_call | solution.py:369
  24.8 0.1 collective-permute-done.1
  24.9 10.0 %all_to_all.21.got_ref = bf16[32,16,128]{2,1,0:T(8,128)(2,1)S(1)} all-to-all(bf16[32,16,128]{2,1,0:T(8,128)(2,1)S(1)} %bitcast.13), channel_id=1, replica_groups=mesh['mem'=4,'grid'=8] {'mem','grid'}, dimensions={0} | all-to-all | bytes 262144 | tf_op jit(solution)/shard_map/all_to_all | solution.py:332
  34.9 0.1 middle.1
  35.1 9.9 %all_to_all.22 = bf16[32,16,128]{2,1,0:T(8,128)(2,1)S(1)} all-to-all(bf16[32,16,128]{2,1,0:T(8,128)(2,1)S(1)} %get-tuple-element.25), channel_id=1, replica_groups=mesh['mem'=4,'grid'=8] {'mem','grid'}, dimensions={0} | all-to-all | bytes 262144 | tf_op jit(solution)/shard_map/all_to_all | solution.py:332
  45.0 0.2 collective-permute-start.2
  45.1 0.5 sums.1.acc_ref
  45.7 0.6 collective-permute-done.2.po_ref
  46.3 3.3 %second.1 = (f32[512,128]{1,0:T(8,128)S(1)}, f32[32,128,128]{2,1,0:T(8,128)S(1)}, f32[8,128]{1,0:T(8,128)S(1)}, f32[8,128]{1,0:T(8,128)S(1)}) custom-call(f32[2,32,128,512]{3,2,1,0:T(8,128)S(1)} %get-tuple-element.18.ens_ref, f32[32,128,128]{2,1,0:T(8,128)S(1)} %sums.1.acc_ref, bf16[512,128]{1,0:T(8,128)(2,1)S(1)} %bitcast.8, ...), custom_call_target="tpu_custom_call" | custom-call | flops 8388608 | tf_op jit(solution)/shard_map/second/pallas_call | solution.py:378
  49.6 0.3 collective-permute-start.3
  49.8 1.1 %own.3 = f32[512,128]{1,0:T(8,128)S(1)} custom-call(f32[2,32,128,512]{3,2,1,0:T(8,128)S(1)} %get-tuple-element.18.ens_ref, f32[32,128,128]{2,1,0:T(8,128)S(1)} %get-tuple-element.28.wide_ref), custom_call_target="tpu_custom_call" | custom-call | flops 8388608 | tf_op jit(solution)/shard_map/own/pallas_call | solution.py:386
  50.9 0.3 collective-permute-done.3
  51.3 10.9 %all_to_all.23.got_ref = bf16[32,24,128]{2,1,0:T(8,128)(2,1)S(1)} all-to-all(bf16[32,24,128]{2,1,0:T(8,128)(2,1)S(1)} %pad_maximum_fusion), channel_id=1, replica_groups=mesh['mem'=4,'grid'=8] {'mem','grid'}, dimensions={0} | all-to-all | bytes 393216 | tf_op jit(solution)/shard_map/all_to_all | solution.py:332
  62.2 0.7 %last.1 = (f32[4,1024]{1,0:T(4,128)}, f32[4,1024]{1,0:T(4,128)}) custom-call(bf16[32,24,128]{2,1,0:T(8,128)(2,1)S(1)} %all_to_all.23.got_ref, f32[8,128]{1,0:T(8,128)S(1)} %get-tuple-element.31.scal_ref, f32[32,128]{1,0:T(8,128)S(1)} %get-tuple-element.23.direct_ref, f32[32,128]{1,0:T(8,128)S(1)} %get-tuple-element.24.obs_ref, ...), custom_call_target="tpu_custom_call" | custom-call | tf_op jit(solution)/shard_map/last/pallas_call | solution.py:392
  (6 shorter events, 0.1 us)
Async XLA Ops:
  0.6 0.7 %copy-start = (f32[4,1024]{1,0:T(4,128)S(1)}, f32[4,1024]{1,0:T(4,128)}, u32[]{:S(2)}) copy-start(f32[4,1024]{1,0:T(4,128)} %right_ref.1) | copy-start | bytes 49156
  16.5 4.0 %collective-permute-start = (bf16[512,128]{1,0:T(8,128)(2,1)S(1)}, bf16[512,128]{1,0:T(8,128)(2,1)S(1)}, u32[]{:S(2)}, u32[]{:S(2)}) collective-permute-start(bf16[512,128]{1,0:T(8,128)(2,1)S(1)} %bitcast.6), channel_id=1, source_target_pairs={{0,1},{1,0},{2,3},{3,2},{4,5},{5,4},{6,7},{7,6},{8,9},{9,8},{10,11... | collective-permute-start | bytes 393224 | tf_op jit(solution)/shard_map/ppermute | solution.py:329
  23.3 1.6 %collective-permute-start.1 = (f32[512,128]{1,0:T(8,128)S(1)}, f32[512,128]{1,0:T(8,128)S(1)}, u32[]{:S(2)}, u32[]{:S(2)}) collective-permute-start(f32[512,128]{1,0:T(8,128)S(1)} %get-tuple-element.22), channel_id=1, source_target_pairs={{0,1},{1,0},{2,3},{3,2},{4,5},{5,4},{6,7},{7,6},{8,9},{9,8},{10,11... | collective-permute-start | bytes 786440 | tf_op jit(solution)/shard_map/ppermute | solution.py:329
  45.0 1.3 %collective-permute-start.2 = (bf16[512,128]{1,0:T(8,128)(2,1)S(1)}, bf16[512,128]{1,0:T(8,128)(2,1)S(1)}, u32[]{:S(2)}, u32[]{:S(2)}) collective-permute-start(bf16[512,128]{1,0:T(8,128)(2,1)S(1)} %bitcast.9), channel_id=1, source_target_pairs={{0,1},{1,0},{2,3},{3,2},{4,5},{5,4},{6,7},{7,6},{8,9},{9,8},{10,11... | collective-permute-start | bytes 393224 | tf_op jit(solution)/shard_map/ppermute | solution.py:329
  49.6 1.6 %collective-permute-start.3 = (f32[512,128]{1,0:T(8,128)S(1)}, f32[512,128]{1,0:T(8,128)S(1)}, u32[]{:S(2)}, u32[]{:S(2)}) collective-permute-start(f32[512,128]{1,0:T(8,128)S(1)} %get-tuple-element.29), channel_id=1, source_target_pairs={{0,1},{1,0},{2,3},{3,2},{4,5},{5,4},{6,7},{7,6},{8,9},{9,8},{10,11... | collective-permute-start | bytes 786440 | tf_op jit(solution)/shard_map/ppermute | solution.py:329

commit v3 on v2

--- a/solution.py
+++ b/solution.py
@@ -11,7 +11,7 @@
 M = 1024
 LANES = 128
 ROWS = 16
-KEEP = 0.25
+KEEP = 0.125
 REACH = 3
 SHIFTS = range(-REACH, REACH + 1)
 F32 = jnp.float32
@@ -56,7 +56,7 @@
     members, blocks, cells = ens_hbm.shape
     half = cells // 2
     core = core_index()
-    groups = blocks // ROWS
+    chunks = blocks // ROWS
 
     def copies(g):
         span = pl.ds(pl.multiple_of(g * ROWS, ROWS), ROWS)
@@ -80,7 +80,7 @@
             copy.start()
         return 0
 
-    lax.fori_loop(0, groups, begin, 0)
+    lax.fori_loop(0, chunks, begin, 0)
     mine[...] = mine_ref[...].astype(F32)
     for copy in lists:
         copy.wait()
@@ -115,33 +115,38 @@
                 ens_ref[1, k, pl.ds(first, ROWS), cells] = held[1, k, pl.ds(first, ROWS), cells].astype(F32)
         return 0
 
-    lax.fori_loop(0, groups, group, 0)
+    lax.fori_loop(0, chunks, group, 0)
+
+
+def groups(blocks, rows, unroll, body):
+    def group(g, _):
+        body(g * rows if isinstance(g, int) else pl.multiple_of(g * rows, rows))
+        return 0
+
+    lax.fori_loop(0, blocks // rows, group, 0, unroll=unroll)
 
 
 def own_sums_kernel(tiles, ens_ref, mine_ref, acc_ref, mine):
     _, members, blocks, _ = ens_ref.shape
     mine[...] = mine_ref[...].astype(F32)
 
-    def group(g, _):
-        first = pl.multiple_of(g * ROWS, ROWS)
-        parts = [every(mine, t, first, ROWS, tiles) for t in range(tiles)]
+    def body(first):
+        parts = [every(mine, t, first, 8, tiles) for t in range(tiles)]
         for k in range(members):
             acc = None
             for t in range(tiles):
-                term = ens_ref[0, k, pl.ds(first, ROWS), pl.ds(t * LANES, LANES)] * parts[t]
+                term = ens_ref[0, k, pl.ds(first, 8), pl.ds(t * LANES, LANES)] * parts[t]
                 acc = term if acc is None else acc + term
-            acc_ref[k, pl.ds(first, ROWS), :] = acc
-        return 0
-
-    lax.fori_loop(0, blocks // ROWS, group, 0)
+            acc_ref[k, pl.ds(first, 8), :] = acc
+
+    groups(blocks, 8, 16, body)
 
 
 def block_sums(ens_ref, acc_ref, field, sums_ref, tiles):
     _, members, blocks, _ = ens_ref.shape
     lane = lax.broadcasted_iota(jnp.int32, (ROWS, LANES), 1)
 
-    def group(g, _):
-        first = pl.multiple_of(g * ROWS, ROWS)
+    def body(first):
         parts = [every(field, t, first, ROWS, tiles) for t in range(tiles)]
         out = jnp.zeros((ROWS, LANES), F32)
         for k in range(members):
@@ -150,9 +155,8 @@
                 acc = acc + ens_ref[1, k, pl.ds(first, ROWS), pl.ds(t * LANES, LANES)] * parts[t]
             out = jnp.where(lane == k, jnp.sum(acc, axis=1, keepdims=True), out)
         sums_ref[pl.ds(first, ROWS), :] = out
-        return 0
-
-    lax.fori_loop(0, blocks // ROWS, group, 0)
+
+    groups(blocks, ROWS, 8, body)
 
 
 def mixed(sums, pad_ref, share_ref):
@@ -168,25 +172,24 @@
 
 def half_spread(ens_ref, slot, coeff, wide_ref, out_ref, tiles):
     _, members, blocks, _ = ens_ref.shape
-
-    def group(g, _):
-        first = pl.multiple_of(g * ROWS, ROWS)
-        here = None if coeff is None else coeff[pl.ds(first, ROWS), :]
+    rows, unroll = (8, 16) if coeff is None else (64, 1)
+
+    def body(first):
+        here = None if coeff is None else coeff[pl.ds(first, rows), :]
         acc = [None] * tiles
         for k in range(members):
             if here is None:
-                one = wide_ref[k, pl.ds(first, ROWS), :]
+                one = wide_ref[k, pl.ds(first, rows), :]
             else:
-                one = jnp.broadcast_to(here[:, k : k + 1], (ROWS, LANES))
-                wide_ref[k, pl.ds(first, ROWS), :] = one
+                one = jnp.broadcast_to(here[:, k : k + 1], (rows, LANES))
+                wide_ref[k, pl.ds(first, rows), :] = one
             for t in range(tiles):
-                term = ens_ref[slot, k, pl.ds(first, ROWS), pl.ds(t * LANES, LANES)] * one
+                term = ens_ref[slot, k, pl.ds(first, rows), pl.ds(t * LANES, LANES)] * one
                 acc[t] = term if acc[t] is None else acc[t] + term
         for t in range(tiles):
-            out_ref[pl.ds(first * tiles + t, ROWS, stride=tiles), :] = acc[t]
-        return 0
-
-    lax.fori_loop(0, blocks // ROWS, group, 0)
+            out_ref[pl.ds(first * tiles + t, rows, stride=tiles), :] = acc[t]
+
+    groups(blocks, rows, unroll, body)
 
 
 def first_kernel(tiles, ens_ref, acc_ref, other_ref, share_ref, send_ref, sums_ref, wide_ref, other, pad_ref, coeff_ref):
@@ -218,7 +221,7 @@
     q = obs_ref[...] * direct + received(got_ref, rows) * (1.0 / M)
     q_ref[...] = q
     d = direct.astype(BF16).astype(F32)
-    dd = jnp.sum(d * d, axis=1, keepdims=True)
+    dd = jnp.sum(direct * d, axis=1, keepdims=True)
     qd = jnp.sum(d * q, axis=1, keepdims=True)
     row = lax.broadcasted_iota(jnp.int32, dd.shape, 0) % rows // tiles
     tau = jnp.zeros_like(dd)
@@ -228,7 +231,7 @@
         prod = jnp.sum(jnp.where(here, qd, 0.0), axis=0, keepdims=True)
         share = jnp.where(self > 0.0, (1.0 - KEEP) * prod / jnp.where(self > 0.0, self, 1.0), 0.0)
         tau = jnp.where(here, share, tau)
-    spread_out((q - tau * d).astype(BF16), sent_ref)
+    spread_out((q - tau * direct).astype(BF16), sent_ref)
 
 
 def second_kernel(

time: 63.2 us -> 61 us (0.965)
  Pallas kernels: 13.4 us -> 10.1 us
  waiting for transfers between devices: 1 us -> 2.07 us
    pallas_call x1, Pallas kernels: 3.28 us -> 2.15 us  [per_device(): call(part(second_kernel, tiles), 'second', (part_half, lanes, small, smal...]
    pallas_call x1, Pallas kernels: 2.78 us -> 1.69 us  [per_device(): call(part(first_kernel, tiles), 'first', (part_half, table, lanes), [VMEM...]
    ppermute x4, waiting for transfers between devices: 1 us -> 2.07 us  [swap(): return lax.ppermute(x, AXES, pairs)]
    pallas_call x2, Pallas kernels: 2.15 us -> 1.14 us  [per_device(): call(part(own_kernel, tiles), 'own', (part_half,), [VMEM] * 2, mib=mib, c...]
  transfers between devices with their start and end apart: 4 -> 4, of which waited for: 3 -> 3; matrix products, arithmetic and copies ran while one was open for 0% -> 0% of each run, Pallas kernels for 10% -> 9%
where the time goes in v3:
time: 61 us; the launch traced here: 60.7 us
  blocking collectives  46 us (75%)
  Pallas kernels  10.1 us (17%)
  waiting for transfers between devices  2.07 us (3%)
  starting transfers between devices  1.03 us (2%)
  local copies, waits for them, and re-layouts  0.72 us (1%)
  between operations  0.72 us (1%)
    all_to_all x4, blocking collectives, exchange(): return lax.all_to_all(x, AXES, split_axis=0, concat_axis=0, tiled=True)  46 us
    pallas_call x1, Pallas kernels, per_device(): call(part(load_kernel, tiles), 'load', (shape((2, members, blocks, cells...  3.81 us
    pallas_call x1, Pallas kernels, per_device(): call(part(second_kernel, tiles), 'second', (part_half, lanes, small, smal...  2.15 us
    ppermute x4, waiting for transfers between devices, swap(): return lax.ppermute(x, AXES, pairs)  2.07 us
    pallas_call x1, Pallas kernels, per_device(): call(part(first_kernel, tiles), 'first', (part_half, table, lanes), [VMEM...  1.69 us
  transfers between devices with their start and end apart: 4, of which 3 were waited for; matrix products, arithmetic and copies ran while one was open for 0% of the time, Pallas kernels for 9%

profile of v3, /device:TPU:1, one launch (start us, length us, event | category | flops | bytes accessed | tf_op | source)
XLA Modules:
  0.0 60.7 jit_solution(2613292467226614258)
XLA Ops:
  0.6 0.0 copy-start
  0.6 0.7 %copy-done = f32[4,1024]{1,0:T(4,128)S(1)} copy-done((f32[4,1024]{1,0:T(4,128)S(1)}, f32[4,1024]{1,0:T(4,128)}, u32[]{:S(2)}) %copy-start) | copy-done | bytes 16408
  1.4 15.1 %all_to_all.20 = bf16[32,16,128]{2,1,0:T(8,128)(2,1)S(1)} all-to-all(bf16[32,16,128]{2,1,0:T(8,128)(2,1)S(1)} %get-tuple-element.17), channel_id=1, replica_groups=mesh['mem'=4,'grid'=8] {'mem','grid'}, dimensions={0} | all-to-all | bytes 262144 | tf_op jit(solution)/shard_map/all_to_all | solution.py:335
  16.5 0.2 collective-permute-start
  16.7 3.8 %load.1 = (f32[2,32,128,512]{3,2,1,0:T(8,128)S(1)}, f32[7,128,128]{2,1,0:T(8,128)S(1)}, f32[32,128,128]{2,1,0:T(8,128)S(1)}, f32[32,128]{1,0:T(8,128)S(1)}) custom-call(bf16[32,128,1024]{2,1,0:T(8,128)(2,1)} %ens_hbm.1, s32[8,128]{1,0:T(8,128)} %bitcast.14, f32[8,128]{1,0:T(8,128)} %bitcast.15, f32[4,1024]{1,0:T(4,128)} %obs_hbm.1, bf16[512,128]{1,0:T(8,128)(2,1)S(1)} %bitcast.7), custom_call_target="tpu_custom_call" | custom-call | flops 8388608 | bytes 25165824 | tf_op jit(solution)/shard_map/load/pallas_call | solution.py:349
  20.5 0.0 collective-permute-done.other_ref.do_ref
  20.5 1.7 %first.1 = (f32[512,128]{1,0:T(8,128)S(1)}, f32[128,128]{1,0:T(8,128)S(1)}, f32[32,128,128]{2,1,0:T(8,128)S(1)}) custom-call(f32[2,32,128,512]{3,2,1,0:T(8,128)S(1)} %get-tuple-element.18.ens_ref, f32[32,128,128]{2,1,0:T(8,128)S(1)} %get-tuple-element.19.acc_ref, bf16[512,128]{1,0:T(8,128)(2,1)S(1)} %collective-permute-done.other_ref.do_ref, ...), custom_call_target="tpu_custom_call" | custom-call | flops 8388608 | tf_op jit(solution)/shard_map/first/pallas_call | solution.py:368
  22.2 0.4 collective-permute-start.1
  22.6 0.6 own.2
  23.2 0.6 %collective-permute-done.1 = f32[512,128]{1,0:T(8,128)S(1)} collective-permute-done((f32[512,128]{1,0:T(8,128)S(1)}, f32[512,128]{1,0:T(8,128)S(1)}, u32[]{:S(2)}, u32[]{:S(2)}) %collective-permute-start.1) | collective-permute-done | bytes 262176 | tf_op jit(solution)/shard_map/ppermute | solution.py:332
  23.9 10.0 %all_to_all.21.got_ref = bf16[32,16,128]{2,1,0:T(8,128)(2,1)S(1)} all-to-all(bf16[32,16,128]{2,1,0:T(8,128)(2,1)S(1)} %bitcast.13), channel_id=1, replica_groups=mesh['mem'=4,'grid'=8] {'mem','grid'}, dimensions={0} | all-to-all | bytes 262144 | tf_op jit(solution)/shard_map/all_to_all | solution.py:335
  33.9 0.1 middle.1
  34.0 9.9 %all_to_all.22 = bf16[32,16,128]{2,1,0:T(8,128)(2,1)S(1)} all-to-all(bf16[32,16,128]{2,1,0:T(8,128)(2,1)S(1)} %get-tuple-element.25), channel_id=1, replica_groups=mesh['mem'=4,'grid'=8] {'mem','grid'}, dimensions={0} | all-to-all | bytes 262144 | tf_op jit(solution)/shard_map/all_to_all | solution.py:335
  43.9 0.2 collective-permute-start.2
  44.1 0.5 sums.1.acc_ref
  44.6 0.7 %collective-permute-done.2.po_ref = bf16[512,128]{1,0:T(8,128)(2,1)S(1)} collective-permute-done((bf16[512,128]{1,0:T(8,128)(2,1)S(1)}, bf16[512,128]{1,0:T(8,128)(2,1)S(1)}, u32[]{:S(2)}, u32[]{:S(2)}) %collective-permute-start.2) | collective-permute-done | bytes 131104 | tf_op jit(solution)/shard_map/ppermute | solution.py:332
  45.2 2.2 %second.1 = (f32[512,128]{1,0:T(8,128)S(1)}, f32[32,128,128]{2,1,0:T(8,128)S(1)}, f32[8,128]{1,0:T(8,128)S(1)}, f32[8,128]{1,0:T(8,128)S(1)}) custom-call(f32[2,32,128,512]{3,2,1,0:T(8,128)S(1)} %get-tuple-element.18.ens_ref, f32[32,128,128]{2,1,0:T(8,128)S(1)} %sums.1.acc_ref, bf16[512,128]{1,0:T(8,128)(2,1)S(1)} %bitcast.8, ...), custom_call_target="tpu_custom_call" | custom-call | flops 8388608 | tf_op jit(solution)/shard_map/second/pallas_call | solution.py:381
  47.4 0.3 collective-permute-start.3
  47.6 0.6 own.3
  48.2 0.8 %collective-permute-done.3 = f32[512,128]{1,0:T(8,128)S(1)} collective-permute-done((f32[512,128]{1,0:T(8,128)S(1)}, f32[512,128]{1,0:T(8,128)S(1)}, u32[]{:S(2)}, u32[]{:S(2)}) %collective-permute-start.3) | collective-permute-done | bytes 262176 | tf_op jit(solution)/shard_map/ppermute | solution.py:332
  49.1 10.9 %all_to_all.23.got_ref = bf16[32,24,128]{2,1,0:T(8,128)(2,1)S(1)} all-to-all(bf16[32,24,128]{2,1,0:T(8,128)(2,1)S(1)} %pad_maximum_fusion), channel_id=1, replica_groups=mesh['mem'=4,'grid'=8] {'mem','grid'}, dimensions={0} | all-to-all | bytes 393216 | tf_op jit(solution)/shard_map/all_to_all | solution.py:335
  60.0 0.7 %last.1 = (f32[4,1024]{1,0:T(4,128)}, f32[4,1024]{1,0:T(4,128)}) custom-call(bf16[32,24,128]{2,1,0:T(8,128)(2,1)S(1)} %all_to_all.23.got_ref, f32[8,128]{1,0:T(8,128)S(1)} %get-tuple-element.31.scal_ref, f32[32,128]{1,0:T(8,128)S(1)} %get-tuple-element.23.direct_ref, f32[32,128]{1,0:T(8,128)S(1)} %get-tuple-element.24.obs_ref, ...), custom_call_target="tpu_custom_call" | custom-call | tf_op jit(solution)/shard_map/last/pallas_call | solution.py:395
  (6 shorter events, 0.1 us)
Async XLA Ops:
  0.6 0.7 %copy-start = (f32[4,1024]{1,0:T(4,128)S(1)}, f32[4,1024]{1,0:T(4,128)}, u32[]{:S(2)}) copy-start(f32[4,1024]{1,0:T(4,128)} %right_ref.1) | copy-start | bytes 49156
  16.5 4.0 %collective-permute-start = (bf16[512,128]{1,0:T(8,128)(2,1)S(1)}, bf16[512,128]{1,0:T(8,128)(2,1)S(1)}, u32[]{:S(2)}, u32[]{:S(2)}) collective-permute-start(bf16[512,128]{1,0:T(8,128)(2,1)S(1)} %bitcast.6), channel_id=1, source_target_pairs={{0,1},{1,0},{2,3},{3,2},{4,5},{5,4},{6,7},{7,6},{8,9},{9,8},{10,11... | collective-permute-start | bytes 393224 | tf_op jit(solution)/shard_map/ppermute | solution.py:332
  22.2 1.6 %collective-permute-start.1 = (f32[512,128]{1,0:T(8,128)S(1)}, f32[512,128]{1,0:T(8,128)S(1)}, u32[]{:S(2)}, u32[]{:S(2)}) collective-permute-start(f32[512,128]{1,0:T(8,128)S(1)} %get-tuple-element.22), channel_id=1, source_target_pairs={{0,1},{1,0},{2,3},{3,2},{4,5},{5,4},{6,7},{7,6},{8,9},{9,8},{10,11... | collective-permute-start | bytes 786440 | tf_op jit(solution)/shard_map/ppermute | solution.py:332
  43.9 1.3 %collective-permute-start.2 = (bf16[512,128]{1,0:T(8,128)(2,1)S(1)}, bf16[512,128]{1,0:T(8,128)(2,1)S(1)}, u32[]{:S(2)}, u32[]{:S(2)}) collective-permute-start(bf16[512,128]{1,0:T(8,128)(2,1)S(1)} %bitcast.9), channel_id=1, source_target_pairs={{0,1},{1,0},{2,3},{3,2},{4,5},{5,4},{6,7},{7,6},{8,9},{9,8},{10,11... | collective-permute-start | bytes 393224 | tf_op jit(solution)/shard_map/ppermute | solution.py:332
  47.4 1.6 %collective-permute-start.3 = (f32[512,128]{1,0:T(8,128)S(1)}, f32[512,128]{1,0:T(8,128)S(1)}, u32[]{:S(2)}, u32[]{:S(2)}) collective-permute-start(f32[512,128]{1,0:T(8,128)S(1)} %get-tuple-element.29), channel_id=1, source_target_pairs={{0,1},{1,0},{2,3},{3,2},{4,5},{5,4},{6,7},{7,6},{8,9},{9,8},{10,11... | collective-permute-start | bytes 786440 | tf_op jit(solution)/shard_map/ppermute | solution.py:332

commit v4 on v3

--- a/solution.py
+++ b/solution.py
@@ -50,21 +50,22 @@
 
 
 def load_kernel(
-    tiles, ens_hbm, nbr_hbm, weight_hbm, obs_hbm, mine_ref, ens_ref, share_ref, acc_ref, obs_ref,
-    held, mine, nbr_ref, weight_ref, laid, sems, small,
+    tiles, ens_hbm, nbr_hbm, weight_hbm, obs_hbm, mine_ref, ens_ref, share_ref, acc_ref, obs_ref, mine,
+    held, nbr_ref, weight_ref, laid, sems, small,
 ):
     members, blocks, cells = ens_hbm.shape
     half = cells // 2
     core = core_index()
-    chunks = blocks // ROWS
-
-    def copies(g):
-        span = pl.ds(pl.multiple_of(g * ROWS, ROWS), ROWS)
+    each = sems.shape[1]
+    chunks, each = each, members // each
+
+    def copies(c):
+        span = pl.ds(c * each, each)
         out = []
         for slot in range(2):
             col = pl.multiple_of(lax.rem(core + slot, 2) * half, half)
-            source = ens_hbm.at[:, span, pl.ds(col, half)]
-            out.append(pltpu.make_async_copy(source, held.at[slot, :, span], sems.at[slot, g]))
+            source = ens_hbm.at[span, :, pl.ds(col, half)]
+            out.append(pltpu.make_async_copy(source, held.at[slot, span], sems.at[slot, c]))
         return out
 
     lists = (
@@ -75,8 +76,8 @@
     for copy in lists:
         copy.start()
 
-    def begin(g, _):
-        for copy in copies(g):
+    def begin(c, _):
+        for copy in copies(c):
             copy.start()
         return 0
 
@@ -97,25 +98,30 @@
     for i in range(len(SHIFTS)):
         share_ref[i] = jnp.broadcast_to(shares[:, i : i + 1], (blocks, LANES))
 
-    def group(g, _):
-        first = pl.multiple_of(g * ROWS, ROWS)
-        for copy in copies(g):
+    def chunk(c, _):
+        for copy in copies(c):
             copy.wait()
-        parts = [every(mine, t, first, ROWS, tiles) for t in range(tiles)]
-        for k in range(members):
-            acc = None
-            for t in range(tiles):
-                cells = pl.ds(t * LANES, LANES)
-                one = held[0, k, pl.ds(first, ROWS), cells].astype(F32)
-                ens_ref[0, k, pl.ds(first, ROWS), cells] = one
-                acc = one * parts[t] if acc is None else acc + one * parts[t]
-            acc_ref[k, pl.ds(first, ROWS), :] = acc
-            for t in range(tiles):
-                cells = pl.ds(t * LANES, LANES)
-                ens_ref[1, k, pl.ds(first, ROWS), cells] = held[1, k, pl.ds(first, ROWS), cells].astype(F32)
+
+        def body(first):
+            here = pl.ds(first, ROWS)
+            parts = [every(mine, t, first, ROWS, tiles) for t in range(tiles)]
+            for i in range(each):
+                k = c * each + i
+                acc = None
+                for t in range(tiles):
+                    cells = pl.ds(t * LANES, LANES)
+                    one = held[0, k, here, cells].astype(F32)
+                    ens_ref[0, k, here, cells] = one
+                    acc = one * parts[t] if acc is None else acc + one * parts[t]
+                acc_ref[k, here, :] = acc
+                for t in range(tiles):
+                    cells = pl.ds(t * LANES, LANES)
+                    ens_ref[1, k, here, cells] = held[1, k, here, cells].astype(F32)
+
+        groups(blocks, ROWS, 8, body)
         return 0
 
-    lax.fori_loop(0, chunks, group, 0)
+    lax.fori_loop(0, chunks, chunk, 0)
 
 
 def groups(blocks, rows, unroll, body):
@@ -126,23 +132,27 @@
     lax.fori_loop(0, blocks // rows, group, 0, unroll=unroll)
 
 
-def own_sums_kernel(tiles, ens_ref, mine_ref, acc_ref, mine):
+def own_sums_kernel(tiles, ens_ref, mine_ref, dm_ref, do_ref, acc_ref, dd_ref, pd_ref, pp_ref, mine):
     _, members, blocks, _ = ens_ref.shape
     mine[...] = mine_ref[...].astype(F32)
 
     def body(first):
+        here = pl.ds(first, 8)
         parts = [every(mine, t, first, 8, tiles) for t in range(tiles)]
         for k in range(members):
-            acc = None
-            for t in range(tiles):
-                term = ens_ref[0, k, pl.ds(first, 8), pl.ds(t * LANES, LANES)] * parts[t]
-                acc = term if acc is None else acc + term
-            acc_ref[k, pl.ds(first, 8), :] = acc
+            acc_ref[k, here, :] = sum(
+                ens_ref[0, k, here, pl.ds(t * LANES, LANES)] * parts[t] for t in range(tiles)
+            )
+        own = [every(dm_ref, t, first, 8, tiles) for t in range(tiles)]
+        far = [every(do_ref, t, first, 8, tiles) for t in range(tiles)]
+        dd_ref[here, :] = sum(d * d for d in own + far)
+        pd_ref[here, :] = sum(p * d for p, d in zip(parts, own))
+        pp_ref[here, :] = sum(p * p for p in parts)
 
     groups(blocks, 8, 16, body)
 
 
-def block_sums(ens_ref, acc_ref, field, sums_ref, tiles):
+def block_sums(ens_ref, acc_ref, field, sums_ref, tiles, also=None):
     _, members, blocks, _ = ens_ref.shape
     lane = lax.broadcasted_iota(jnp.int32, (ROWS, LANES), 1)
 
@@ -155,6 +165,8 @@
                 acc = acc + ens_ref[1, k, pl.ds(first, ROWS), pl.ds(t * LANES, LANES)] * parts[t]
             out = jnp.where(lane == k, jnp.sum(acc, axis=1, keepdims=True), out)
         sums_ref[pl.ds(first, ROWS), :] = out
+        if also is not None:
+            also(first, parts)
 
     groups(blocks, ROWS, 8, body)
 
@@ -172,7 +184,7 @@
 
 def half_spread(ens_ref, slot, coeff, wide_ref, out_ref, tiles):
     _, members, blocks, _ = ens_ref.shape
-    rows, unroll = (8, 16) if coeff is None else (64, 1)
+    rows, unroll = (8, 16) if coeff is None else (16, 8)
 
     def body(first):
         here = None if coeff is None else coeff[pl.ds(first, rows), :]
@@ -181,7 +193,7 @@
             if here is None:
                 one = wide_ref[k, pl.ds(first, rows), :]
             else:
-                one = jnp.broadcast_to(here[:, k : k + 1], (rows, LANES))
+                one = jnp.broadcast_to(here[:, k : k + 1].astype(BF16), (rows, LANES)).astype(F32)
                 wide_ref[k, pl.ds(first, rows), :] = one
             for t in range(tiles):
                 term = ens_ref[slot, k, pl.ds(first, rows), pl.ds(t * LANES, LANES)] * one
@@ -235,48 +247,50 @@
 
 
 def second_kernel(
-    tiles, ens_ref, acc_ref, dm_ref, do_ref, pm_ref, po_ref, share_ref, sums0_ref, direct_ref, q_ref, obs_ref,
-    send_ref, wide_ref, scal_ref, extra_ref, mine, other, dm, do, sums_ref, pad_ref, coeff_ref,
+    tiles, ens_ref, acc_ref, dd_ref, pd_ref, pp_ref, do_ref, po_ref, share_ref, sums0_ref,
+    send_ref, wide_ref, scal_ref, sums_ref, coeff_ref, other, pd_all, pp_all, pad_ref,
 ):
     blocks = ens_ref.shape[2]
-    mine[...] = pm_ref[...].astype(F32)
     other[...] = po_ref[...].astype(F32)
-    dm[...] = dm_ref[...].astype(F32)
-    do[...] = do_ref[...].astype(F32)
-    block_sums(ens_ref, acc_ref, other, sums_ref, tiles)
-    prod = jnp.zeros((blocks, LANES), F32)
-    self = jnp.zeros((blocks, LANES), F32)
-    halves = ((dm, mine), (do, other))
-    for d_ref, p_ref in halves:
-        for t in range(tiles):
-            d = every(d_ref, t, 0, blocks, tiles)
-            prod = prod + d * every(p_ref, t, 0, blocks, tiles)
-            self = self + d * d
-    pd = jnp.sum(prod, axis=1, keepdims=True)
-    dd = jnp.sum(self, axis=1, keepdims=True)
+
+    def products(first):
+        here = pl.ds(first, ROWS)
+        parts = [every(other, t, first, ROWS, tiles) for t in range(tiles)]
+        far = [every(do_ref, t, first, ROWS, tiles) for t in range(tiles)]
+        pd_all[here, :] = pd_ref[here, :] + sum(p * d for p, d in zip(parts, far))
+        pp_all[here, :] = pp_ref[here, :] + sum(p * p for p in parts)
+
+    groups(blocks, ROWS, 8, products)
+    dd = jnp.sum(dd_ref[...], axis=1, keepdims=True)
+    pd = jnp.sum(pd_all[...], axis=1, keepdims=True)
+    pp = jnp.sum(pp_all[...], axis=1, keepdims=True)
     tau = jnp.where(dd > 0.0, (1.0 / KEEP - 1.0) * pd / jnp.where(dd > 0.0, dd, 1.0), 0.0)
     rr0 = jnp.sum(dd, axis=0, keepdims=True)
     alpha = rr0 / jnp.sum(pd + tau * dd, axis=0, keepdims=True)
     keep = 1.0 - alpha * tau
-    left = jnp.zeros((blocks, LANES), F32)
-    for d_ref, p_ref in halves:
-        for t in range(tiles):
-            r = keep * every(d_ref, t, 0, blocks, tiles) - alpha * every(p_ref, t, 0, blocks, tiles)
-            left = left + r * r
-    rr1 = jnp.sum(jnp.sum(left, axis=1, keepdims=True), axis=0, keepdims=True)
+    rr1 = jnp.sum(keep * (keep * dd - 2.0 * alpha * pd) + alpha * alpha * pp, axis=0, keepdims=True)
     beta = rr1 / rr0
+    row = lax.broadcasted_iota(jnp.int32, (8, LANES), 0)
+    scal_ref[...] = jnp.where(row == 0, alpha, jnp.where(row == 1, beta, rr1))
+    block_sums(ens_ref, acc_ref, other, sums_ref, tiles)
     sums = (beta + keep) * sums0_ref[...] - alpha * sums_ref[...]
-    coeff = mixed(sums, pad_ref, share_ref)
-    coeff_ref[...] = coeff
+    sums_ref[...] = sums
+    coeff_ref[...] = mixed(sums, pad_ref, share_ref)
+    half_spread(ens_ref, 1, coeff_ref, wide_ref, send_ref, tiles)
+
+
+def second_own_kernel(
+    tiles, ens_ref, wide_ref, sums_ref, coeff_ref, scal_ref, direct_ref, q_ref, obs_ref, own_ref, extra_ref
+):
+    alpha, beta = scal_ref[0:1, :], scal_ref[1:2, :]
     direction = (1.0 + beta) * direct_ref[...] - alpha * q_ref[...]
-    part = jnp.sum(jnp.sum(sums * coeff, axis=0, keepdims=True), axis=1, keepdims=True) * (1.0 / M)
+    part = jnp.sum(jnp.sum(sums_ref[...] * coeff_ref[...], axis=0, keepdims=True), axis=1, keepdims=True) * (1.0 / M)
     part += jnp.sum(jnp.sum(obs_ref[...] * direction * direction, axis=0, keepdims=True), axis=1, keepdims=True)
     row = lax.broadcasted_iota(jnp.int32, (8, LANES), 0)
-    scal_ref[...] = jnp.where(row == 0, alpha, jnp.where(row == 1, beta, rr1))
     high = part.astype(BF16).astype(F32)
     mid = (part - high).astype(BF16).astype(F32)
     extra_ref[...] = jnp.where(row == 0, high, jnp.where(row == 1, mid, jnp.where(row == 2, part - high - mid, 0.0)))
-    half_spread(ens_ref, 1, coeff_ref, wide_ref, send_ref, tiles)
+    half_spread(ens_ref, 0, None, wide_ref, own_ref, tiles)
 
 
 def last_kernel(tiles, got_ref, scal_ref, direct_ref, obs_ref, q_ref, solution_ref, residual_ref, sol, res):
@@ -346,18 +360,17 @@
     sent, direct = call(part(start_kernel, tiles), "start", (to_all, mine), [VMEM])(right_side)
     d_mine = exchange(sent).reshape(half, LANES)
     d_other = swap(d_mine)
-    ens, share, acc, obs = call(
+    ens, share, acc, obs, d_mine = call(
         part(load_kernel, tiles),
         "load",
-        (shape((2, members, blocks, cells // 2), F32), shape((len(SHIFTS), blocks, LANES), F32), lanes, mine),
+        (shape((2, members, blocks, cells // 2), F32), shape((len(SHIFTS), blocks, LANES), F32), lanes, mine, part_half),
         [HBM, HBM, HBM, HBM, VMEM],
         [
             pltpu.VMEM((2, members, blocks, cells // 2), BF16),
-            field,
             pltpu.VMEM(neighbors.shape[::-1], jnp.int32),
             pltpu.VMEM(loc_weight.shape[::-1], F32),
             pltpu.VMEM((own, cells), F32),
-            pltpu.SemaphoreType.DMA((2, blocks // ROWS)),
+            pltpu.SemaphoreType.DMA((2, members // 2)),
             pltpu.SemaphoreType.DMA((3,)),
         ],
         mib=8 + mib,
@@ -365,8 +378,8 @@
     )(*(pltpu.with_memory_space_constraint(x, pltpu.HBM) for x in (ensemble, neighbors.T, loc_weight.T, obs_prec)), d_mine)
 
     coeffs = pltpu.VMEM((blocks, LANES), F32)
-    send, sums0, wide = call(
-        part(first_kernel, tiles), "first", (part_half, table, lanes), [VMEM] * 4, [field, padded, coeffs],
+    send, sums0, wide, d_other = call(
+        part(first_kernel, tiles), "first", (part_half, table, lanes, part_half), [VMEM] * 4, [padded, coeffs],
         mib=mib, cost=(work, 0),
     )(ens, acc, d_other, share)
     (kept,) = call(part(own_kernel, tiles), "own", (part_half,), [VMEM] * 2, mib=mib, cost=(work, 0))(ens, wide)
@@ -377,16 +390,21 @@
     p_other = swap(p_mine)
 
     small = shape((8, LANES), F32)
-    (acc,) = call(part(own_sums_kernel, tiles), "sums", (lanes,), [VMEM] * 2, [field], mib=mib, cost=(work, 0))(ens, p_mine)
-    send, wide, scal, extra = call(
+    acc, dd, pd, pp = call(
+        part(own_sums_kernel, tiles), "sums", (lanes, table, table, table), [VMEM] * 4, [field], mib=mib, cost=(work, 0)
+    )(ens, p_mine, d_mine, d_other)
+    send, wide, scal, sums, coeff = call(
         part(second_kernel, tiles),
         "second",
-        (part_half, lanes, small, small),
-        [VMEM] * 11,
-        [field] * 4 + [coeffs, padded, coeffs],
-        mib=mib, cost=(work, 0),
-    )(ens, acc, d_mine, d_other, p_mine, p_other, share, sums0, direct, q, obs)
-    (kept,) = call(part(own_kernel, tiles), "own", (part_half,), [VMEM] * 2, mib=mib, cost=(work, 0))(ens, wide)
+        (part_half, lanes, small, table, table),
+        [VMEM] * 9,
+        [field, coeffs, coeffs, padded],
+        mib=mib,
+        cost=(work, 0),
+    )(ens, acc, dd, pd, pp, d_other, p_other, share, sums0)
+    kept, extra = call(
+        part(second_own_kernel, tiles), "second_own", (part_half, small), [VMEM] * 8, mib=mib, cost=(work, 0)
+    )(ens, wide, sums, coeff, scal, direct, q, obs)
     both = (kept + swap(send)).reshape(to_all.shape)
     both = jnp.concatenate([both, jnp.broadcast_to(extra[None], (devices, 8, LANES))], axis=1)
     got = exchange(both.astype(BF16))

time: 61 us -> 60.5 us (level)
    pallas_call x3 -> x4, Pallas kernels: 4.33 us -> 4.39 us  [the longest x1 1.75 us: per_device(): call(part(second_kernel, tiles), 'second', (part_half, lanes, small, tabl...]
where the time goes in v4:
time: 60.5 us; the launch traced here: 60.1 us
  blocking collectives  46 us (76%)
  Pallas kernels  9.59 us (16%)
  waiting for transfers between devices  2.01 us (3%)
  starting transfers between devices  1.03 us (2%)
  between operations  0.73 us (1%)
  local copies, waits for them, and re-layouts  0.72 us (1%)
    all_to_all x4, blocking collectives, exchange(): return lax.all_to_all(x, AXES, split_axis=0, concat_axis=0, tiled=True)  46 us
    pallas_call x1, Pallas kernels, per_device(): call(part(load_kernel, tiles), 'load', (shape((2, members, blocks, cells...  3.8 us
    ppermute x4, waiting for transfers between devices, swap(): return lax.ppermute(x, AXES, pairs)  2.01 us
    pallas_call x1, Pallas kernels, per_device(): call(part(second_kernel, tiles), 'second', (part_half, lanes, small, tabl...  1.75 us
    pallas_call x1, Pallas kernels, per_device(): call(part(first_kernel, tiles), 'first', (part_half, table, lanes, part_h...  1.53 us
  transfers between devices with their start and end apart: 4, of which 3 were waited for; matrix products, arithmetic and copies ran while one was open for 0% of the time, Pallas kernels for 9%

profile of v4, /device:TPU:1, one launch (start us, length us, event | category | flops | bytes accessed | tf_op | source)
XLA Modules:
  0.0 60.1 jit_solution(15751534162310674211)
XLA Ops:
  0.6 0.0 copy-start
  0.6 0.7 %copy-done = f32[4,1024]{1,0:T(4,128)S(1)} copy-done((f32[4,1024]{1,0:T(4,128)S(1)}, f32[4,1024]{1,0:T(4,128)}, u32[]{:S(2)}) %copy-start) | copy-done | bytes 16408
  1.4 15.1 %all_to_all.20 = bf16[32,16,128]{2,1,0:T(8,128)(2,1)S(1)} all-to-all(bf16[32,16,128]{2,1,0:T(8,128)(2,1)S(1)} %get-tuple-element.26), channel_id=1, replica_groups=mesh['mem'=4,'grid'=8] {'mem','grid'}, dimensions={0} | all-to-all | bytes 262144 | tf_op jit(solution)/shard_map/all_to_all | solution.py:349
  16.5 0.2 collective-permute-start
  16.7 3.8 %load.1 = (f32[2,32,128,512]{3,2,1,0:T(8,128)S(1)}, f32[7,128,128]{2,1,0:T(8,128)S(1)}, f32[32,128,128]{2,1,0:T(8,128)S(1)}, f32[32,128]{1,0:T(8,128)S(1)}, f32[512,128]{1,0:T(8,128)S(1)}) custom-call(bf16[32,128,1024]{2,1,0:T(8,128)(2,1)} %ens_hbm.1, s32[8,128]{1,0:T(8,128)} %bitcast.12, f32[8,128]{1,0:T(8,128)} %bitcast.13, f32[4,1024]{1,0:T(4,128)} %obs_hbm.1, ...), custom_call_target="tpu_custom_call" | custom-call | flops 8388608 | bytes 25165824 | tf_op jit(solution)/shard_map/load/pallas_call | solution.py:363
  20.5 0.0 collective-permute-done.other_ref
  20.5 1.5 %first.1 = (f32[512,128]{1,0:T(8,128)S(1)}, f32[128,128]{1,0:T(8,128)S(1)}, f32[32,128,128]{2,1,0:T(8,128)S(1)}, f32[512,128]{1,0:T(8,128)S(1)}) custom-call(f32[2,32,128,512]{3,2,1,0:T(8,128)S(1)} %get-tuple-element.27.ens_ref, f32[32,128,128]{2,1,0:T(8,128)S(1)} %get-tuple-element.28.acc_ref, bf16[512,128]{1,0:T(8,128)(2,1)S(1)} %collective-permute-done.other_ref, ...), custom_call_target="tpu_custom_call" | custom-call | flops 8388608 | tf_op jit(solution)/shard_map/first/pallas_call | solution.py:381
  22.1 0.4 collective-permute-start.1
  22.4 0.6 own.1
  23.0 0.6 %collective-permute-done.1 = f32[512,128]{1,0:T(8,128)S(1)} collective-permute-done((f32[512,128]{1,0:T(8,128)S(1)}, f32[512,128]{1,0:T(8,128)S(1)}, u32[]{:S(2)}, u32[]{:S(2)}) %collective-permute-start.1) | collective-permute-done | bytes 262176 | tf_op jit(solution)/shard_map/ppermute | solution.py:346
  23.7 10.0 %all_to_all.21.got_ref = bf16[32,16,128]{2,1,0:T(8,128)(2,1)S(1)} all-to-all(bf16[32,16,128]{2,1,0:T(8,128)(2,1)S(1)} %bitcast.11), channel_id=1, replica_groups=mesh['mem'=4,'grid'=8] {'mem','grid'}, dimensions={0} | all-to-all | bytes 262144 | tf_op jit(solution)/shard_map/all_to_all | solution.py:349
  33.7 0.1 middle.1
  33.8 9.9 %all_to_all.22 = bf16[32,16,128]{2,1,0:T(8,128)(2,1)S(1)} all-to-all(bf16[32,16,128]{2,1,0:T(8,128)(2,1)S(1)} %get-tuple-element.34), channel_id=1, replica_groups=mesh['mem'=4,'grid'=8] {'mem','grid'}, dimensions={0} | all-to-all | bytes 262144 | tf_op jit(solution)/shard_map/all_to_all | solution.py:349
  43.7 0.2 collective-permute-start.2
  43.9 0.6 sums.1
  44.5 0.6 collective-permute-done.2.po_ref
  45.1 1.8 %second.1 = (f32[512,128]{1,0:T(8,128)S(1)}, f32[32,128,128]{2,1,0:T(8,128)S(1)}, f32[8,128]{1,0:T(8,128)S(1)}, f32[128,128]{1,0:T(8,128)S(1)}, f32[128,128]{1,0:T(8,128)S(1)}) custom-call(f32[2,32,128,512]{3,2,1,0:T(8,128)S(1)} %get-tuple-element.27.ens_ref, f32[32,128,128]{2,1,0:T(8,128)S(1)} %get-tuple-element.37.acc_ref, ...), custom_call_target="tpu_custom_call" | custom-call | flops 8388608 | tf_op jit(solution)/shard_map/second/pallas_call | solution.py:396
  46.8 0.3 collective-permute-start.3
  47.1 0.6 second_own.1
  47.6 0.8 %collective-permute-done.3 = f32[512,128]{1,0:T(8,128)S(1)} collective-permute-done((f32[512,128]{1,0:T(8,128)S(1)}, f32[512,128]{1,0:T(8,128)S(1)}, u32[]{:S(2)}, u32[]{:S(2)}) %collective-permute-start.3) | collective-permute-done | bytes 262176 | tf_op jit(solution)/shard_map/ppermute | solution.py:346
  48.5 10.9 %all_to_all.23.got_ref = bf16[32,24,128]{2,1,0:T(8,128)(2,1)S(1)} all-to-all(bf16[32,24,128]{2,1,0:T(8,128)(2,1)S(1)} %pad_maximum_fusion), channel_id=1, replica_groups=mesh['mem'=4,'grid'=8] {'mem','grid'}, dimensions={0} | all-to-all | bytes 393216 | tf_op jit(solution)/shard_map/all_to_all | solution.py:349
  59.4 0.7 %last.1 = (f32[4,1024]{1,0:T(4,128)}, f32[4,1024]{1,0:T(4,128)}) custom-call(bf16[32,24,128]{2,1,0:T(8,128)(2,1)S(1)} %all_to_all.23.got_ref, f32[8,128]{1,0:T(8,128)S(1)} %get-tuple-element.45.scal_ref, f32[32,128]{1,0:T(8,128)S(1)} %get-tuple-element.32.direct_ref, f32[32,128]{1,0:T(8,128)S(1)} %get-tuple-element.33.obs_ref, ...), custom_call_target="tpu_custom_call" | custom-call | tf_op jit(solution)/shard_map/last/pallas_call | solution.py:413
  (6 shorter events, 0.1 us)
Async XLA Ops:
  0.6 0.7 %copy-start = (f32[4,1024]{1,0:T(4,128)S(1)}, f32[4,1024]{1,0:T(4,128)}, u32[]{:S(2)}) copy-start(f32[4,1024]{1,0:T(4,128)} %right_ref.1) | copy-start | bytes 49156
  16.5 4.0 %collective-permute-start = (bf16[512,128]{1,0:T(8,128)(2,1)S(1)}, bf16[512,128]{1,0:T(8,128)(2,1)S(1)}, u32[]{:S(2)}, u32[]{:S(2)}) collective-permute-start(bf16[512,128]{1,0:T(8,128)(2,1)S(1)} %bitcast.8), channel_id=1, source_target_pairs={{0,1},{1,0},{2,3},{3,2},{4,5},{5,4},{6,7},{7,6},{8,9},{9,8},{10,11... | collective-permute-start | bytes 393224 | tf_op jit(solution)/shard_map/ppermute | solution.py:346
  22.1 1.6 %collective-permute-start.1 = (f32[512,128]{1,0:T(8,128)S(1)}, f32[512,128]{1,0:T(8,128)S(1)}, u32[]{:S(2)}, u32[]{:S(2)}) collective-permute-start(f32[512,128]{1,0:T(8,128)S(1)} %get-tuple-element.31), channel_id=1, source_target_pairs={{0,1},{1,0},{2,3},{3,2},{4,5},{5,4},{6,7},{7,6},{8,9},{9,8},{10,11... | collective-permute-start | bytes 786440 | tf_op jit(solution)/shard_map/ppermute | solution.py:346
  43.7 1.3 %collective-permute-start.2 = (bf16[512,128]{1,0:T(8,128)(2,1)S(1)}, bf16[512,128]{1,0:T(8,128)(2,1)S(1)}, u32[]{:S(2)}, u32[]{:S(2)}) collective-permute-start(bf16[512,128]{1,0:T(8,128)(2,1)S(1)} %bitcast.6), channel_id=1, source_target_pairs={{0,1},{1,0},{2,3},{3,2},{4,5},{5,4},{6,7},{7,6},{8,9},{9,8},{10,11... | collective-permute-start | bytes 393224 | tf_op jit(solution)/shard_map/ppermute | solution.py:346
  46.8 1.6 %collective-permute-start.3 = (f32[512,128]{1,0:T(8,128)S(1)}, f32[512,128]{1,0:T(8,128)S(1)}, u32[]{:S(2)}, u32[]{:S(2)}) collective-permute-start(f32[512,128]{1,0:T(8,128)S(1)} %get-tuple-element.48), channel_id=1, source_target_pairs={{0,1},{1,0},{2,3},{3,2},{4,5},{5,4},{6,7},{7,6},{8,9},{9,8},{10,11... | collective-permute-start | bytes 786440 | tf_op jit(solution)/shard_map/ppermute | solution.py:346

commit v5 on v4

--- a/solution.py
+++ b/solution.py
@@ -204,11 +204,12 @@
     groups(blocks, rows, unroll, body)
 
 
-def first_kernel(tiles, ens_ref, acc_ref, other_ref, share_ref, send_ref, sums_ref, wide_ref, other, pad_ref, coeff_ref):
+def first_kernel(tiles, ens_ref, acc_ref, other_ref, share_ref, send_ref, sums_ref, wide_ref, other, pad_ref, coeff_ref, spread):
     other[...] = other_ref[...].astype(F32)
     block_sums(ens_ref, acc_ref, other, sums_ref, tiles)
     coeff_ref[...] = mixed(sums_ref[...], pad_ref, share_ref)
-    half_spread(ens_ref, 1, coeff_ref, wide_ref, send_ref, tiles)
+    half_spread(ens_ref, 1, coeff_ref, wide_ref, spread, tiles)
+    send_ref[...] = spread[...].astype(BF16)
 
 
 def own_kernel(tiles, ens_ref, wide_ref, own_ref):
@@ -248,7 +249,7 @@
 
 def second_kernel(
     tiles, ens_ref, acc_ref, dd_ref, pd_ref, pp_ref, do_ref, po_ref, share_ref, sums0_ref,
-    send_ref, wide_ref, scal_ref, sums_ref, coeff_ref, other, pd_all, pp_all, pad_ref,
+    send_ref, wide_ref, scal_ref, sums_ref, coeff_ref, other, pd_all, pp_all, pad_ref, spread,
 ):
     blocks = ens_ref.shape[2]
     other[...] = po_ref[...].astype(F32)
@@ -276,7 +277,8 @@
     sums = (beta + keep) * sums0_ref[...] - alpha * sums_ref[...]
     sums_ref[...] = sums
     coeff_ref[...] = mixed(sums, pad_ref, share_ref)
-    half_spread(ens_ref, 1, coeff_ref, wide_ref, send_ref, tiles)
+    half_spread(ens_ref, 1, coeff_ref, wide_ref, spread, tiles)
+    send_ref[...] = spread[...].astype(BF16)
 
 
 def second_own_kernel(
@@ -351,6 +353,7 @@
     to_all = shape((devices, rows, LANES), BF16)
     lanes = shape((members, blocks, LANES), F32)
     table = shape((blocks, LANES), F32)
+    to_swap = shape((half, LANES), BF16)
     part_half = shape((half, LANES), F32)
     mine = shape((2 * rows, LANES), F32)
     field = pltpu.VMEM((half, LANES), F32)
@@ -379,11 +382,11 @@
 
     coeffs = pltpu.VMEM((blocks, LANES), F32)
     send, sums0, wide, d_other = call(
-        part(first_kernel, tiles), "first", (part_half, table, lanes, part_half), [VMEM] * 4, [padded, coeffs],
+        part(first_kernel, tiles), "first", (to_swap, table, lanes, part_half), [VMEM] * 4, [padded, coeffs, field],
         mib=mib, cost=(work, 0),
     )(ens, acc, d_other, share)
     (kept,) = call(part(own_kernel, tiles), "own", (part_half,), [VMEM] * 2, mib=mib, cost=(work, 0))(ens, wide)
-    got = exchange((kept + swap(send)).astype(BF16).reshape(to_all.shape))
+    got = exchange((kept + swap(send).astype(F32)).astype(BF16).reshape(to_all.shape))
 
     q, sent = call(part(middle_kernel, tiles), "middle", (mine, to_all), [VMEM] * 3)(got, direct, obs)
     p_mine = exchange(sent).reshape(half, LANES)
@@ -396,16 +399,16 @@
     send, wide, scal, sums, coeff = call(
         part(second_kernel, tiles),
         "second",
-        (part_half, lanes, small, table, table),
+        (to_swap, lanes, small, table, table),
         [VMEM] * 9,
-        [field, coeffs, coeffs, padded],
+        [field, coeffs, coeffs, padded, field],
         mib=mib,
         cost=(work, 0),
     )(ens, acc, dd, pd, pp, d_other, p_other, share, sums0)
     kept, extra = call(
         part(second_own_kernel, tiles), "second_own", (part_half, small), [VMEM] * 8, mib=mib, cost=(work, 0)
     )(ens, wide, sums, coeff, scal, direct, q, obs)
-    both = (kept + swap(send)).reshape(to_all.shape)
+    both = (kept + swap(send).astype(F32)).reshape(to_all.shape)
     both = jnp.concatenate([both, jnp.broadcast_to(extra[None], (devices, 8, LANES))], axis=1)
     got = exchange(both.astype(BF16))
     out = shape((own, cells), F32)

time: 60.5 us -> 60.1 us (level)
  no operation moved by 1% of the time
where the time goes in v5:
time: 60.1 us; the launch traced here: 59.8 us
  blocking collectives  46 us (77%)
  Pallas kernels  9.6 us (16%)
  waiting for transfers between devices  1.64 us (3%)
  starting transfers between devices  1.03 us (2%)
  local copies, waits for them, and re-layouts  0.72 us (1%)
  between operations  0.72 us (1%)
    all_to_all x4, blocking collectives, exchange(): return lax.all_to_all(x, AXES, split_axis=0, concat_axis=0, tiled=True)  46 us
    pallas_call x1, Pallas kernels, per_device(): call(part(load_kernel, tiles), 'load', (shape((2, members, blocks, cells...  3.8 us
    pallas_call x1, Pallas kernels, per_device(): call(part(second_kernel, tiles), 'second', (to_swap, lanes, small, table,...  1.76 us
    ppermute x4, waiting for transfers between devices, swap(): return lax.ppermute(x, AXES, pairs)  1.64 us
    pallas_call x1, Pallas kernels, per_device(): call(part(first_kernel, tiles), 'first', (to_swap, table, lanes, part_hal...  1.54 us
  transfers between devices with their start and end apart: 4, of which 3 were waited for; matrix products, arithmetic and copies ran while one was open for 0% of the time, Pallas kernels for 9%

profile of v5, /device:TPU:1, one launch (start us, length us, event | category | flops | bytes accessed | tf_op | source)
XLA Modules:
  0.0 59.8 jit_solution(17996624336874539407)
XLA Ops:
  0.6 0.0 copy-start
  0.6 0.7 %copy-done = f32[4,1024]{1,0:T(4,128)S(1)} copy-done((f32[4,1024]{1,0:T(4,128)S(1)}, f32[4,1024]{1,0:T(4,128)}, u32[]{:S(2)}) %copy-start) | copy-done | bytes 16408
  1.4 15.1 %all_to_all.20 = bf16[32,16,128]{2,1,0:T(8,128)(2,1)S(1)} all-to-all(bf16[32,16,128]{2,1,0:T(8,128)(2,1)S(1)} %get-tuple-element.26), channel_id=1, replica_groups=mesh['mem'=4,'grid'=8] {'mem','grid'}, dimensions={0} | all-to-all | bytes 262144 | tf_op jit(solution)/shard_map/all_to_all | solution.py:351
  16.5 0.2 collective-permute-start
  16.7 3.8 %load.1 = (f32[2,32,128,512]{3,2,1,0:T(8,128)S(1)}, f32[7,128,128]{2,1,0:T(8,128)S(1)}, f32[32,128,128]{2,1,0:T(8,128)S(1)}, f32[32,128]{1,0:T(8,128)S(1)}, f32[512,128]{1,0:T(8,128)S(1)}) custom-call(bf16[32,128,1024]{2,1,0:T(8,128)(2,1)} %ens_hbm.1, s32[8,128]{1,0:T(8,128)} %bitcast.12, f32[8,128]{1,0:T(8,128)} %bitcast.13, f32[4,1024]{1,0:T(4,128)} %obs_hbm.1, ...), custom_call_target="tpu_custom_call" | custom-call | flops 8388608 | bytes 25165824 | tf_op jit(solution)/shard_map/load/pallas_call | solution.py:366
  20.5 0.0 collective-permute-done.other_ref
  20.5 1.5 %first.1 = (bf16[512,128]{1,0:T(8,128)(2,1)S(1)}, f32[128,128]{1,0:T(8,128)S(1)}, f32[32,128,128]{2,1,0:T(8,128)S(1)}, f32[512,128]{1,0:T(8,128)S(1)}) custom-call(f32[2,32,128,512]{3,2,1,0:T(8,128)S(1)} %get-tuple-element.27.ens_ref, f32[32,128,128]{2,1,0:T(8,128)S(1)} %get-tuple-element.28.acc_ref, bf16[512,128]{1,0:T(8,128)(2,1)S(1)} %collective-permute-done.other_ref, ...), custom_call_target="tpu_custom_call" | custom-call | flops 8388608 | tf_op jit(solution)/shard_map/first/pallas_call | solution.py:384
  22.1 0.4 collective-permute-start.1
  22.5 0.6 own.1
  23.0 0.5 collective-permute-done.1
  23.5 10.0 %all_to_all.21.got_ref = bf16[32,16,128]{2,1,0:T(8,128)(2,1)S(1)} all-to-all(bf16[32,16,128]{2,1,0:T(8,128)(2,1)S(1)} %bitcast.11), channel_id=1, replica_groups=mesh['mem'=4,'grid'=8] {'mem','grid'}, dimensions={0} | all-to-all | bytes 262144 | tf_op jit(solution)/shard_map/all_to_all | solution.py:351
  33.5 0.1 middle.1
  33.6 9.9 %all_to_all.22 = bf16[32,16,128]{2,1,0:T(8,128)(2,1)S(1)} all-to-all(bf16[32,16,128]{2,1,0:T(8,128)(2,1)S(1)} %get-tuple-element.34), channel_id=1, replica_groups=mesh['mem'=4,'grid'=8] {'mem','grid'}, dimensions={0} | all-to-all | bytes 262144 | tf_op jit(solution)/shard_map/all_to_all | solution.py:351
  43.5 0.2 collective-permute-start.2
  43.7 0.6 sums.1
  44.3 0.6 collective-permute-done.2.po_ref
  44.9 1.8 %second.1 = (bf16[512,128]{1,0:T(8,128)(2,1)S(1)}, f32[32,128,128]{2,1,0:T(8,128)S(1)}, f32[8,128]{1,0:T(8,128)S(1)}, f32[128,128]{1,0:T(8,128)S(1)}, f32[128,128]{1,0:T(8,128)S(1)}) custom-call(f32[2,32,128,512]{3,2,1,0:T(8,128)S(1)} %get-tuple-element.27.ens_ref, f32[32,128,128]{2,1,0:T(8,128)S(1)} %get-tuple-element.37.acc_ref, ...), custom_call_target="tpu_custom_call" | custom-call | flops 8388608 | tf_op jit(solution)/shard_map/second/pallas_call | solution.py:399
  46.6 0.3 collective-permute-start.3
  46.9 0.6 second_own.1
  47.5 0.6 collective-permute-done.3
  48.1 10.9 %all_to_all.23.got_ref = bf16[32,24,128]{2,1,0:T(8,128)(2,1)S(1)} all-to-all(bf16[32,24,128]{2,1,0:T(8,128)(2,1)S(1)} %pad_maximum_fusion), channel_id=1, replica_groups=mesh['mem'=4,'grid'=8] {'mem','grid'}, dimensions={0} | all-to-all | bytes 393216 | tf_op jit(solution)/shard_map/all_to_all | solution.py:351
  59.1 0.7 %last.1 = (f32[4,1024]{1,0:T(4,128)}, f32[4,1024]{1,0:T(4,128)}) custom-call(bf16[32,24,128]{2,1,0:T(8,128)(2,1)S(1)} %all_to_all.23.got_ref, f32[8,128]{1,0:T(8,128)S(1)} %get-tuple-element.45.scal_ref, f32[32,128]{1,0:T(8,128)S(1)} %get-tuple-element.32.direct_ref, f32[32,128]{1,0:T(8,128)S(1)} %get-tuple-element.33.obs_ref, ...), custom_call_target="tpu_custom_call" | custom-call | tf_op jit(solution)/shard_map/last/pallas_call | solution.py:416
  (6 shorter events, 0.1 us)
Async XLA Ops:
  0.6 0.7 %copy-start = (f32[4,1024]{1,0:T(4,128)S(1)}, f32[4,1024]{1,0:T(4,128)}, u32[]{:S(2)}) copy-start(f32[4,1024]{1,0:T(4,128)} %right_ref.1) | copy-start | bytes 49156
  16.5 4.0 %collective-permute-start = (bf16[512,128]{1,0:T(8,128)(2,1)S(1)}, bf16[512,128]{1,0:T(8,128)(2,1)S(1)}, u32[]{:S(2)}, u32[]{:S(2)}) collective-permute-start(bf16[512,128]{1,0:T(8,128)(2,1)S(1)} %bitcast.8), channel_id=1, source_target_pairs={{0,1},{1,0},{2,3},{3,2},{4,5},{5,4},{6,7},{7,6},{8,9},{9,8},{10,11... | collective-permute-start | bytes 393224 | tf_op jit(solution)/shard_map/ppermute | solution.py:348
  22.1 1.4 %collective-permute-start.1 = (bf16[512,128]{1,0:T(8,128)(2,1)S(1)}, bf16[512,128]{1,0:T(8,128)(2,1)S(1)}, u32[]{:S(2)}, u32[]{:S(2)}) collective-permute-start(bf16[512,128]{1,0:T(8,128)(2,1)S(1)} %get-tuple-element.31), channel_id=1, source_target_pairs={{0,1},{1,0},{2,3},{3,2},{4,5},{5,4},{6,7},{7,6},{8,9},{9,8},{10,11... | collective-permute-start | bytes 393224 | tf_op jit(solution)/shard_map/ppermute | solution.py:348
  43.5 1.3 %collective-permute-start.2 = (bf16[512,128]{1,0:T(8,128)(2,1)S(1)}, bf16[512,128]{1,0:T(8,128)(2,1)S(1)}, u32[]{:S(2)}, u32[]{:S(2)}) collective-permute-start(bf16[512,128]{1,0:T(8,128)(2,1)S(1)} %bitcast.6), channel_id=1, source_target_pairs={{0,1},{1,0},{2,3},{3,2},{4,5},{5,4},{6,7},{7,6},{8,9},{9,8},{10,11... | collective-permute-start | bytes 393224 | tf_op jit(solution)/shard_map/ppermute | solution.py:348
  46.6 1.4 %collective-permute-start.3 = (bf16[512,128]{1,0:T(8,128)(2,1)S(1)}, bf16[512,128]{1,0:T(8,128)(2,1)S(1)}, u32[]{:S(2)}, u32[]{:S(2)}) collective-permute-start(bf16[512,128]{1,0:T(8,128)(2,1)S(1)} %get-tuple-element.48), channel_id=1, source_target_pairs={{0,1},{1,0},{2,3},{3,2},{4,5},{5,4},{6,7},{7,6},{8,9},{9,8},{10,11... | collective-permute-start | bytes 393224 | tf_op jit(solution)/shard_map/ppermute | solution.py:348

commit v6 on v5

--- a/solution.py
+++ b/solution.py
@@ -98,6 +98,9 @@
     for i in range(len(SHIFTS)):
         share_ref[i] = jnp.broadcast_to(shares[:, i : i + 1], (blocks, LANES))
 
+    acc_ref[...] = jnp.zeros_like(acc_ref)
+    lane = lax.broadcasted_iota(jnp.int32, (ROWS, LANES), 1)
+
     def chunk(c, _):
         for copy in copies(c):
             copy.wait()
@@ -105,6 +108,7 @@
         def body(first):
             here = pl.ds(first, ROWS)
             parts = [every(mine, t, first, ROWS, tiles) for t in range(tiles)]
+            sums = acc_ref[here, :]
             for i in range(each):
                 k = c * each + i
                 acc = None
@@ -113,10 +117,11 @@
                     one = held[0, k, here, cells].astype(F32)
                     ens_ref[0, k, here, cells] = one
                     acc = one * parts[t] if acc is None else acc + one * parts[t]
-                acc_ref[k, here, :] = acc
+                sums = jnp.where(lane == k, jnp.sum(acc, axis=1, keepdims=True), sums)
                 for t in range(tiles):
                     cells = pl.ds(t * LANES, LANES)
                     ens_ref[1, k, here, cells] = held[1, k, here, cells].astype(F32)
+            acc_ref[here, :] = sums
 
         groups(blocks, ROWS, 8, body)
         return 0
@@ -133,16 +138,14 @@
 
 
 def own_sums_kernel(tiles, ens_ref, mine_ref, dm_ref, do_ref, acc_ref, dd_ref, pd_ref, pp_ref, mine):
-    _, members, blocks, _ = ens_ref.shape
+    blocks = ens_ref.shape[2]
     mine[...] = mine_ref[...].astype(F32)
+
+    half_sums(ens_ref, 0, mine, acc_ref, tiles)
 
     def body(first):
         here = pl.ds(first, 8)
         parts = [every(mine, t, first, 8, tiles) for t in range(tiles)]
-        for k in range(members):
-            acc_ref[k, here, :] = sum(
-                ens_ref[0, k, here, pl.ds(t * LANES, LANES)] * parts[t] for t in range(tiles)
-            )
         own = [every(dm_ref, t, first, 8, tiles) for t in range(tiles)]
         far = [every(do_ref, t, first, 8, tiles) for t in range(tiles)]
         dd_ref[here, :] = sum(d * d for d in own + far)
@@ -152,21 +155,21 @@
     groups(blocks, 8, 16, body)
 
 
-def block_sums(ens_ref, acc_ref, field, sums_ref, tiles, also=None):
+def half_sums(ens_ref, slot, field, sums_ref, tiles, start=None):
     _, members, blocks, _ = ens_ref.shape
     lane = lax.broadcasted_iota(jnp.int32, (ROWS, LANES), 1)
 
     def body(first):
+        here = pl.ds(first, ROWS)
         parts = [every(field, t, first, ROWS, tiles) for t in range(tiles)]
         out = jnp.zeros((ROWS, LANES), F32)
         for k in range(members):
-            acc = acc_ref[k, pl.ds(first, ROWS), :]
+            acc = None
             for t in range(tiles):
-                acc = acc + ens_ref[1, k, pl.ds(first, ROWS), pl.ds(t * LANES, LANES)] * parts[t]
+                term = ens_ref[slot, k, here, pl.ds(t * LANES, LANES)] * parts[t]
+                acc = term if acc is None else acc + term
             out = jnp.where(lane == k, jnp.sum(acc, axis=1, keepdims=True), out)
-        sums_ref[pl.ds(first, ROWS), :] = out
-        if also is not None:
-            also(first, parts)
+        sums_ref[here, :] = out if start is None else out + start[here, :]
 
     groups(blocks, ROWS, 8, body)
 
@@ -206,7 +209,7 @@
 
 def first_kernel(tiles, ens_ref, acc_ref, other_ref, share_ref, send_ref, sums_ref, wide_ref, other, pad_ref, coeff_ref, spread):
     other[...] = other_ref[...].astype(F32)
-    block_sums(ens_ref, acc_ref, other, sums_ref, tiles)
+    half_sums(ens_ref, 1, other, sums_ref, tiles, acc_ref)
     coeff_ref[...] = mixed(sums_ref[...], pad_ref, share_ref)
     half_spread(ens_ref, 1, coeff_ref, wide_ref, spread, tiles)
     send_ref[...] = spread[...].astype(BF16)
@@ -273,7 +276,7 @@
     beta = rr1 / rr0
     row = lax.broadcasted_iota(jnp.int32, (8, LANES), 0)
     scal_ref[...] = jnp.where(row == 0, alpha, jnp.where(row == 1, beta, rr1))
-    block_sums(ens_ref, acc_ref, other, sums_ref, tiles)
+    half_sums(ens_ref, 1, other, sums_ref, tiles, acc_ref)
     sums = (beta + keep) * sums0_ref[...] - alpha * sums_ref[...]
     sums_ref[...] = sums
     coeff_ref[...] = mixed(sums, pad_ref, share_ref)
@@ -366,14 +369,14 @@
     ens, share, acc, obs, d_mine = call(
         part(load_kernel, tiles),
         "load",
-        (shape((2, members, blocks, cells // 2), F32), shape((len(SHIFTS), blocks, LANES), F32), lanes, mine, part_half),
+        (shape((2, members, blocks, cells // 2), F32), shape((len(SHIFTS), blocks, LANES), F32), table, mine, part_half),
         [HBM, HBM, HBM, HBM, VMEM],
         [
             pltpu.VMEM((2, members, blocks, cells // 2), BF16),
             pltpu.VMEM(neighbors.shape[::-1], jnp.int32),
             pltpu.VMEM(loc_weight.shape[::-1], F32),
             pltpu.VMEM((own, cells), F32),
-            pltpu.SemaphoreType.DMA((2, members // 2)),
+            pltpu.SemaphoreType.DMA((2, members // 4)),
             pltpu.SemaphoreType.DMA((3,)),
         ],
         mib=8 + mib,
@@ -394,7 +397,7 @@
 
     small = shape((8, LANES), F32)
     acc, dd, pd, pp = call(
-        part(own_sums_kernel, tiles), "sums", (lanes, table, table, table), [VMEM] * 4, [field], mib=mib, cost=(work, 0)
+        part(own_sums_kernel, tiles), "sums", (table, table, table, table), [VMEM] * 4, [field], mib=mib, cost=(work, 0)
     )(ens, p_mine, d_mine, d_other)
     send, wide, scal, sums, coeff = call(
         part(second_kernel, tiles),

time: 60.1 us -> 59.8 us (level)
  transfers between devices with their start and end apart: 4 -> 4, of which waited for: 3 -> 3; matrix products, arithmetic and copies ran while one was open for 0% -> 0% of each run, Pallas kernels for 9% -> 10%
where the time goes in v6:
time: 59.8 us; the launch traced here: 59.5 us
  blocking collectives  46 us (77%)
  Pallas kernels  9.66 us (16%)
  waiting for transfers between devices  1.31 us (2%)
  starting transfers between devices  1.03 us (2%)
  local copies, waits for them, and re-layouts  0.72 us (1%)
  between operations  0.71 us (1%)
    all_to_all x4, blocking collectives, exchange(): return lax.all_to_all(x, AXES, split_axis=0, concat_axis=0, tiled=True)  46 us
    pallas_call x1, Pallas kernels, per_device(): call(part(load_kernel, tiles), 'load', (shape((2, members, blocks, cells...  3.82 us
    pallas_call x1, Pallas kernels, per_device(): call(part(second_kernel, tiles), 'second', (to_swap, lanes, small, table,...  1.55 us
    pallas_call x1, Pallas kernels, per_device(): call(part(first_kernel, tiles), 'first', (to_swap, table, lanes, part_hal...  1.46 us
    ppermute x4, waiting for transfers between devices, swap(): return lax.ppermute(x, AXES, pairs)  1.31 us
  transfers between devices with their start and end apart: 4, of which 3 were waited for; matrix products, arithmetic and copies ran while one was open for 0% of the time, Pallas kernels for 10%

profile of v6, /device:TPU:1, one launch (start us, length us, event | category | flops | bytes accessed | tf_op | source)
XLA Modules:
  0.0 59.5 jit_solution(16929372661612104370)
XLA Ops:
  0.6 0.0 copy-start
  0.6 0.7 %copy-done = f32[4,1024]{1,0:T(4,128)S(1)} copy-done((f32[4,1024]{1,0:T(4,128)S(1)}, f32[4,1024]{1,0:T(4,128)}, u32[]{:S(2)}) %copy-start) | copy-done | bytes 16408
  1.4 15.1 %all_to_all.20 = bf16[32,16,128]{2,1,0:T(8,128)(2,1)S(1)} all-to-all(bf16[32,16,128]{2,1,0:T(8,128)(2,1)S(1)} %get-tuple-element.26), channel_id=1, replica_groups=mesh['mem'=4,'grid'=8] {'mem','grid'}, dimensions={0} | all-to-all | bytes 262144 | tf_op jit(solution)/shard_map/all_to_all | solution.py:354
  16.5 0.2 collective-permute-start
  16.7 3.8 %load.1 = (f32[2,32,128,512]{3,2,1,0:T(8,128)S(1)}, f32[7,128,128]{2,1,0:T(8,128)S(1)}, f32[128,128]{1,0:T(8,128)S(1)}, f32[32,128]{1,0:T(8,128)S(1)}, f32[512,128]{1,0:T(8,128)S(1)}) custom-call(bf16[32,128,1024]{2,1,0:T(8,128)(2,1)} %ens_hbm.1, s32[8,128]{1,0:T(8,128)} %bitcast.12, f32[8,128]{1,0:T(8,128)} %bitcast.13, f32[4,1024]{1,0:T(4,128)} %obs_hbm.1, ...), custom_call_target="tpu_custom_call" | custom-call | flops 8388608 | bytes 25165824 | tf_op jit(solution)/shard_map/load/pallas_call | solution.py:369
  20.5 0.0 collective-permute-done.other_ref
  20.5 1.5 %first.1 = (bf16[512,128]{1,0:T(8,128)(2,1)S(1)}, f32[128,128]{1,0:T(8,128)S(1)}, f32[32,128,128]{2,1,0:T(8,128)S(1)}, f32[512,128]{1,0:T(8,128)S(1)}) custom-call(f32[2,32,128,512]{3,2,1,0:T(8,128)S(1)} %get-tuple-element.27.ens_ref, f32[128,128]{1,0:T(8,128)S(1)} %get-tuple-element.28.acc_ref, bf16[512,128]{1,0:T(8,128)(2,1)S(1)} %collective-permute-done.other_ref, ...), custom_call_target="tpu_custom_call" | custom-call | flops 8388608 | tf_op jit(solution)/shard_map/first/pallas_call | solution.py:387
  22.0 0.4 collective-permute-start.1
  22.4 0.6 own.1
  23.0 0.5 collective-permute-done.1
  23.5 10.0 %all_to_all.21.got_ref = bf16[32,16,128]{2,1,0:T(8,128)(2,1)S(1)} all-to-all(bf16[32,16,128]{2,1,0:T(8,128)(2,1)S(1)} %bitcast.11), channel_id=1, replica_groups=mesh['mem'=4,'grid'=8] {'mem','grid'}, dimensions={0} | all-to-all | bytes 262144 | tf_op jit(solution)/shard_map/all_to_all | solution.py:354
  33.4 0.1 middle.1
  33.6 9.9 %all_to_all.22 = bf16[32,16,128]{2,1,0:T(8,128)(2,1)S(1)} all-to-all(bf16[32,16,128]{2,1,0:T(8,128)(2,1)S(1)} %get-tuple-element.34), channel_id=1, replica_groups=mesh['mem'=4,'grid'=8] {'mem','grid'}, dimensions={0} | all-to-all | bytes 262144 | tf_op jit(solution)/shard_map/all_to_all | solution.py:354
  43.5 0.2 collective-permute-start.2
  43.7 0.7 %sums.1 = (f32[128,128]{1,0:T(8,128)S(1)}, f32[128,128]{1,0:T(8,128)S(1)}, f32[128,128]{1,0:T(8,128)S(1)}, f32[128,128]{1,0:T(8,128)S(1)}) custom-call(f32[2,32,128,512]{3,2,1,0:T(8,128)S(1)} %get-tuple-element.27.ens_ref, bf16[512,128]{1,0:T(8,128)(2,1)S(1)} %bitcast.7, f32[512,128]{1,0:T(8,128)S(1)} %get-tuple-element.35.dm_ref, ...), custom_call_target="tpu_custom_call" | custom-call | flops 8388608 | tf_op jit(solution)/shard_map/sums/pallas_call | solution.py:399
  44.4 0.4 collective-permute-done.2.po_ref
  44.8 1.6 %second.1 = (bf16[512,128]{1,0:T(8,128)(2,1)S(1)}, f32[32,128,128]{2,1,0:T(8,128)S(1)}, f32[8,128]{1,0:T(8,128)S(1)}, f32[128,128]{1,0:T(8,128)S(1)}, f32[128,128]{1,0:T(8,128)S(1)}) custom-call(f32[2,32,128,512]{3,2,1,0:T(8,128)S(1)} %get-tuple-element.27.ens_ref, f32[128,128]{1,0:T(8,128)S(1)} %get-tuple-element.37.acc_ref, ...), custom_call_target="tpu_custom_call" | custom-call | flops 8388608 | tf_op jit(solution)/shard_map/second/pallas_call | solution.py:402
  46.4 0.3 collective-permute-start.3
  46.6 0.7 %second_own.1 = (f32[512,128]{1,0:T(8,128)S(1)}, f32[8,128]{1,0:T(8,128)S(1)}) custom-call(f32[2,32,128,512]{3,2,1,0:T(8,128)S(1)} %get-tuple-element.27.ens_ref, f32[32,128,128]{2,1,0:T(8,128)S(1)} %get-tuple-element.42.wide_ref, f32[128,128]{1,0:T(8,128)S(1)} %get-tuple-element.43.sums_ref, f32[128,128]{1,0:T(8,128)S(1)} %get-tuple-element.44.coeff_ref, ...), custom_call_target="tpu_custom_call" | custom-call | flops 8388608 | tf_op jit(solution)/shard_map/second_own/pallas_call | solution.py:411
  47.4 0.4 collective-permute-done.3
  47.9 10.9 %all_to_all.23.got_ref = bf16[32,24,128]{2,1,0:T(8,128)(2,1)S(1)} all-to-all(bf16[32,24,128]{2,1,0:T(8,128)(2,1)S(1)} %pad_maximum_fusion), channel_id=1, replica_groups=mesh['mem'=4,'grid'=8] {'mem','grid'}, dimensions={0} | all-to-all | bytes 393216 | tf_op jit(solution)/shard_map/all_to_all | solution.py:354
  58.8 0.7 %last.1 = (f32[4,1024]{1,0:T(4,128)}, f32[4,1024]{1,0:T(4,128)}) custom-call(bf16[32,24,128]{2,1,0:T(8,128)(2,1)S(1)} %all_to_all.23.got_ref, f32[8,128]{1,0:T(8,128)S(1)} %get-tuple-element.45.scal_ref, f32[32,128]{1,0:T(8,128)S(1)} %get-tuple-element.32.direct_ref, f32[32,128]{1,0:T(8,128)S(1)} %get-tuple-element.33.obs_ref, ...), custom_call_target="tpu_custom_call" | custom-call | tf_op jit(solution)/shard_map/last/pallas_call | solution.py:419
  (6 shorter events, 0.1 us)
Async XLA Ops:
  0.6 0.7 %copy-start = (f32[4,1024]{1,0:T(4,128)S(1)}, f32[4,1024]{1,0:T(4,128)}, u32[]{:S(2)}) copy-start(f32[4,1024]{1,0:T(4,128)} %right_ref.1) | copy-start | bytes 49156
  16.5 4.0 %collective-permute-start = (bf16[512,128]{1,0:T(8,128)(2,1)S(1)}, bf16[512,128]{1,0:T(8,128)(2,1)S(1)}, u32[]{:S(2)}, u32[]{:S(2)}) collective-permute-start(bf16[512,128]{1,0:T(8,128)(2,1)S(1)} %bitcast.8), channel_id=1, source_target_pairs={{0,1},{1,0},{2,3},{3,2},{4,5},{5,4},{6,7},{7,6},{8,9},{9,8},{10,11... | collective-permute-start | bytes 393224 | tf_op jit(solution)/shard_map/ppermute | solution.py:351
  22.0 1.4 %collective-permute-start.1 = (bf16[512,128]{1,0:T(8,128)(2,1)S(1)}, bf16[512,128]{1,0:T(8,128)(2,1)S(1)}, u32[]{:S(2)}, u32[]{:S(2)}) collective-permute-start(bf16[512,128]{1,0:T(8,128)(2,1)S(1)} %get-tuple-element.31), channel_id=1, source_target_pairs={{0,1},{1,0},{2,3},{3,2},{4,5},{5,4},{6,7},{7,6},{8,9},{9,8},{10,11... | collective-permute-start | bytes 393224 | tf_op jit(solution)/shard_map/ppermute | solution.py:351
  43.5 1.3 %collective-permute-start.2 = (bf16[512,128]{1,0:T(8,128)(2,1)S(1)}, bf16[512,128]{1,0:T(8,128)(2,1)S(1)}, u32[]{:S(2)}, u32[]{:S(2)}) collective-permute-start(bf16[512,128]{1,0:T(8,128)(2,1)S(1)} %bitcast.6), channel_id=1, source_target_pairs={{0,1},{1,0},{2,3},{3,2},{4,5},{5,4},{6,7},{7,6},{8,9},{9,8},{10,11... | collective-permute-start | bytes 393224 | tf_op jit(solution)/shard_map/ppermute | solution.py:351
  46.4 1.4 %collective-permute-start.3 = (bf16[512,128]{1,0:T(8,128)(2,1)S(1)}, bf16[512,128]{1,0:T(8,128)(2,1)S(1)}, u32[]{:S(2)}, u32[]{:S(2)}) collective-permute-start(bf16[512,128]{1,0:T(8,128)(2,1)S(1)} %get-tuple-element.48), channel_id=1, source_target_pairs={{0,1},{1,0},{2,3},{3,2},{4,5},{5,4},{6,7},{7,6},{8,9},{9,8},{10,11... | collective-permute-start | bytes 393224 | tf_op jit(solution)/shard_map/ppermute | solution.py:351

commit v7 on v6

--- a/solution.py
+++ b/solution.py
@@ -292,24 +292,22 @@
     part = jnp.sum(jnp.sum(sums_ref[...] * coeff_ref[...], axis=0, keepdims=True), axis=1, keepdims=True) * (1.0 / M)
     part += jnp.sum(jnp.sum(obs_ref[...] * direction * direction, axis=0, keepdims=True), axis=1, keepdims=True)
     row = lax.broadcasted_iota(jnp.int32, (8, LANES), 0)
+    lane = lax.broadcasted_iota(jnp.int32, (8, LANES), 1)
     high = part.astype(BF16).astype(F32)
     mid = (part - high).astype(BF16).astype(F32)
-    extra_ref[...] = jnp.where(row == 0, high, jnp.where(row == 1, mid, jnp.where(row == 2, part - high - mid, 0.0)))
+    extra_ref[...] = jnp.where(row == 0, jnp.where(lane < LANES // 2, high, mid), part - high - mid)
     half_spread(ens_ref, 0, None, wide_ref, own_ref, tiles)
 
 
-def last_kernel(tiles, got_ref, scal_ref, direct_ref, obs_ref, q_ref, solution_ref, residual_ref, sol, res):
-    devices, rows, _ = got_ref.shape
-    rows -= 8
-    denom = jnp.zeros((8, LANES), F32)
-    for i in range(devices):
-        denom = denom + got_ref[i, rows:, :].astype(F32)
-    denom = jnp.sum(denom, axis=0, keepdims=True)
+def last_kernel(tiles, spread_ref, extra_ref, scal_ref, direct_ref, obs_ref, q_ref, solution_ref, residual_ref, sol, res):
+    rows = spread_ref.shape[0] // 2
+    parts = extra_ref[0] + extra_ref[1]
+    denom = jnp.sum(parts[0:1], axis=1, keepdims=True) * (2.0 / LANES) + parts[1:2]
     alpha, beta, rr1 = scal_ref[0:1, :], scal_ref[1:2, :], scal_ref[2:3, :]
     direct = direct_ref[...]
     residual = direct - alpha * q_ref[...]
     direction = residual + beta * direct
-    image = obs_ref[...] * direction + received(got_ref, rows) * (1.0 / M)
+    image = obs_ref[...] * direction + spread_ref[...] * (1.0 / M)
     alpha1 = rr1 / denom
     sol[...] = alpha * direct + alpha1 * direction
     res[...] = residual - alpha1 * image
@@ -411,12 +409,15 @@
     kept, extra = call(
         part(second_own_kernel, tiles), "second_own", (part_half, small), [VMEM] * 8, mib=mib, cost=(work, 0)
     )(ens, wide, sums, coeff, scal, direct, q, obs)
-    both = (kept + swap(send).astype(F32)).reshape(to_all.shape)
-    both = jnp.concatenate([both, jnp.broadcast_to(extra[None], (devices, 8, LANES))], axis=1)
-    got = exchange(both.astype(BF16))
+    both = (kept + swap(send).astype(F32)).astype(BF16).reshape(devices, rows // 2, 2, LANES)
+    extra = jnp.broadcast_to(extra[:2].astype(BF16).reshape(1, 1, 2, LANES), (devices, 1, 2, LANES))
+    got = exchange(jnp.concatenate([both, extra], axis=1))
+    got = jnp.sum(got.reshape(devices // 2, 2, rows // 2 + 1, 2, LANES).astype(F32), axis=0)
+    spread = got[:, : rows // 2].reshape(2 * rows, LANES)
+    extra = got[:, rows // 2]
     out = shape((own, cells), F32)
     scratch = pltpu.VMEM((2 * rows, LANES), F32)
-    return call(part(last_kernel, tiles), "last", (out, out), [VMEM] * 5, [scratch] * 2)(got, scal, direct, obs, q)
+    return call(part(last_kernel, tiles), "last", (out, out), [VMEM] * 6, [scratch] * 2)(spread, extra, scal, direct, obs, q)
 
 
 def solution(mesh):

time: 59.8 us -> 59.4 us (level)
  blocking collectives: 46 us -> 45.2 us
    all_to_all x4, blocking collectives: 46 us -> 45.2 us  [exchange(): return lax.all_to_all(x, AXES, split_axis=0, concat_axis=0, tiled=True)]
where the time goes in v7:
time: 59.4 us; the launch traced here: 59 us
  blocking collectives  45.2 us (76%)
  Pallas kernels  9.69 us (16%)
  waiting for transfers between devices  1.31 us (2%)
  starting transfers between devices  1.03 us (2%)
  local copies, waits for them, and re-layouts  0.73 us (1%)
  between operations  0.73 us (1%)
    all_to_all x4, blocking collectives, exchange(): return lax.all_to_all(x, AXES, split_axis=0, concat_axis=0, tiled=True)  45.2 us
    pallas_call x1, Pallas kernels, per_device(): call(part(load_kernel, tiles), 'load', (shape((2, members, blocks, cells...  3.82 us
    pallas_call x1, Pallas kernels, per_device(): call(part(second_kernel, tiles), 'second', (to_swap, lanes, small, table,...  1.55 us
    pallas_call x1, Pallas kernels, per_device(): call(part(first_kernel, tiles), 'first', (to_swap, table, lanes, part_hal...  1.46 us
    ppermute x4, waiting for transfers between devices, swap(): return lax.ppermute(x, AXES, pairs)  1.31 us
  transfers between devices with their start and end apart: 4, of which 3 were waited for; matrix products, arithmetic and copies ran while one was open for 0% of the time, Pallas kernels for 10%

profile of v7, /device:TPU:1, one launch (start us, length us, event | category | flops | bytes accessed | tf_op | source)
XLA Modules:
  0.0 59.0 jit_solution(3828125143660046438)
XLA Ops:
  0.6 0.0 copy-start
  0.6 0.7 %copy-done = f32[4,1024]{1,0:T(4,128)S(1)} copy-done((f32[4,1024]{1,0:T(4,128)S(1)}, f32[4,1024]{1,0:T(4,128)}, u32[]{:S(2)}) %copy-start) | copy-done | bytes 16408
  1.4 15.1 %all_to_all.20 = bf16[32,16,128]{2,1,0:T(8,128)(2,1)S(1)} all-to-all(bf16[32,16,128]{2,1,0:T(8,128)(2,1)S(1)} %get-tuple-element.26), channel_id=1, replica_groups=mesh['mem'=4,'grid'=8] {'mem','grid'}, dimensions={0} | all-to-all | bytes 262144 | tf_op jit(solution)/shard_map/all_to_all | solution.py:352
  16.5 0.2 collective-permute-start
  16.7 3.8 %load.1 = (f32[2,32,128,512]{3,2,1,0:T(8,128)S(1)}, f32[7,128,128]{2,1,0:T(8,128)S(1)}, f32[128,128]{1,0:T(8,128)S(1)}, f32[32,128]{1,0:T(8,128)S(1)}, f32[512,128]{1,0:T(8,128)S(1)}) custom-call(bf16[32,128,1024]{2,1,0:T(8,128)(2,1)} %ens_hbm.1, s32[8,128]{1,0:T(8,128)} %bitcast.21, f32[8,128]{1,0:T(8,128)} %bitcast.22, f32[4,1024]{1,0:T(4,128)} %obs_hbm.1, ...), custom_call_target="tpu_custom_call" | custom-call | flops 8388608 | bytes 25165824 | tf_op jit(solution)/shard_map/load/pallas_call | solution.py:367
  20.5 0.0 collective-permute-done.other_ref
  20.5 1.5 %first.1 = (bf16[512,128]{1,0:T(8,128)(2,1)S(1)}, f32[128,128]{1,0:T(8,128)S(1)}, f32[32,128,128]{2,1,0:T(8,128)S(1)}, f32[512,128]{1,0:T(8,128)S(1)}) custom-call(f32[2,32,128,512]{3,2,1,0:T(8,128)S(1)} %get-tuple-element.27.ens_ref, f32[128,128]{1,0:T(8,128)S(1)} %get-tuple-element.28.acc_ref, bf16[512,128]{1,0:T(8,128)(2,1)S(1)} %collective-permute-done.other_ref, ...), custom_call_target="tpu_custom_call" | custom-call | flops 8388608 | tf_op jit(solution)/shard_map/first/pallas_call | solution.py:385
  22.0 0.4 collective-permute-start.1
  22.4 0.6 own.1
  23.0 0.5 collective-permute-done.1
  23.5 10.0 %all_to_all.21.got_ref = bf16[32,16,128]{2,1,0:T(8,128)(2,1)S(1)} all-to-all(bf16[32,16,128]{2,1,0:T(8,128)(2,1)S(1)} %bitcast.20), channel_id=1, replica_groups=mesh['mem'=4,'grid'=8] {'mem','grid'}, dimensions={0} | all-to-all | bytes 262144 | tf_op jit(solution)/shard_map/all_to_all | solution.py:352
  33.4 0.1 middle.1
  33.6 9.9 %all_to_all.22 = bf16[32,16,128]{2,1,0:T(8,128)(2,1)S(1)} all-to-all(bf16[32,16,128]{2,1,0:T(8,128)(2,1)S(1)} %get-tuple-element.34), channel_id=1, replica_groups=mesh['mem'=4,'grid'=8] {'mem','grid'}, dimensions={0} | all-to-all | bytes 262144 | tf_op jit(solution)/shard_map/all_to_all | solution.py:352
  43.5 0.2 collective-permute-start.2
  43.7 0.7 %sums.1 = (f32[128,128]{1,0:T(8,128)S(1)}, f32[128,128]{1,0:T(8,128)S(1)}, f32[128,128]{1,0:T(8,128)S(1)}, f32[128,128]{1,0:T(8,128)S(1)}) custom-call(f32[2,32,128,512]{3,2,1,0:T(8,128)S(1)} %get-tuple-element.27.ens_ref, bf16[512,128]{1,0:T(8,128)(2,1)S(1)} %bitcast.14, f32[512,128]{1,0:T(8,128)S(1)} %get-tuple-element.35.dm_ref, ...), custom_call_target="tpu_custom_call" | custom-call | flops 8388608 | tf_op jit(solution)/shard_map/sums/pallas_call | solution.py:397
  44.4 0.4 collective-permute-done.2.po_ref
  44.8 1.6 %second.1 = (bf16[512,128]{1,0:T(8,128)(2,1)S(1)}, f32[32,128,128]{2,1,0:T(8,128)S(1)}, f32[8,128]{1,0:T(8,128)S(1)}, f32[128,128]{1,0:T(8,128)S(1)}, f32[128,128]{1,0:T(8,128)S(1)}) custom-call(f32[2,32,128,512]{3,2,1,0:T(8,128)S(1)} %get-tuple-element.27.ens_ref, f32[128,128]{1,0:T(8,128)S(1)} %get-tuple-element.37.acc_ref, ...), custom_call_target="tpu_custom_call" | custom-call | flops 8388608 | tf_op jit(solution)/shard_map/second/pallas_call | solution.py:400
  46.4 0.3 collective-permute-start.3
  46.6 0.7 %second_own.1 = (f32[512,128]{1,0:T(8,128)S(1)}, f32[8,128]{1,0:T(8,128)S(1)}) custom-call(f32[2,32,128,512]{3,2,1,0:T(8,128)S(1)} %get-tuple-element.27.ens_ref, f32[32,128,128]{2,1,0:T(8,128)S(1)} %get-tuple-element.42.wide_ref, f32[128,128]{1,0:T(8,128)S(1)} %get-tuple-element.43.sums_ref, f32[128,128]{1,0:T(8,128)S(1)} %get-tuple-element.44.coeff_ref, ...), custom_call_target="tpu_custom_call" | custom-call | flops 8388608 | tf_op jit(solution)/shard_map/second_own/pallas_call | solution.py:409
  47.4 0.4 collective-permute-done.3
  47.8 0.2 pad_maximum_fusion
  48.0 10.1 %all_to_all.23 = bf16[32,9,2,128]{3,2,1,0:T(2,128)(2,1)S(1)} all-to-all(bf16[32,9,2,128]{3,2,1,0:T(2,128)(2,1)S(1)} %pad_maximum_fusion), channel_id=1, replica_groups=mesh['mem'=4,'grid'=8] {'mem','grid'}, dimensions={0} | all-to-all | bytes 294912 | tf_op jit(solution)/shard_map/all_to_all | solution.py:352
  58.2 0.1 convert_reduce_fusion
  58.3 0.7 %last.1 = (f32[4,1024]{1,0:T(4,128)}, f32[4,1024]{1,0:T(4,128)}) custom-call(f32[32,128]{1,0:T(8,128)S(1)} %bitcast.17, f32[2,2,128]{2,1,0:T(2,128)S(1)} %slice_bitcast_fusion.extra_ref, f32[8,128]{1,0:T(8,128)S(1)} %get-tuple-element.45.scal_ref, f32[32,128]{1,0:T(8,128)S(1)} %get-tuple-element.32.direct_ref, f32[32,128]{1,0:T(8,128)S(1)} %get-tuple-element.33.obs_ref, ...), custom_call_target="tpu_custom_call" | custom-call | tf_op jit(solution)/shard_map/last/pallas_call | solution.py:420
  (8 shorter events, 0.1 us)
Async XLA Ops:
  0.6 0.7 %copy-start = (f32[4,1024]{1,0:T(4,128)S(1)}, f32[4,1024]{1,0:T(4,128)}, u32[]{:S(2)}) copy-start(f32[4,1024]{1,0:T(4,128)} %right_ref.1) | copy-start | bytes 49156
  16.5 4.0 %collective-permute-start = (bf16[512,128]{1,0:T(8,128)(2,1)S(1)}, bf16[512,128]{1,0:T(8,128)(2,1)S(1)}, u32[]{:S(2)}, u32[]{:S(2)}) collective-permute-start(bf16[512,128]{1,0:T(8,128)(2,1)S(1)} %bitcast.15), channel_id=1, source_target_pairs={{0,1},{1,0},{2,3},{3,2},{4,5},{5,4},{6,7},{7,6},{8,9},{9,8},{10,11... | collective-permute-start | bytes 393224 | tf_op jit(solution)/shard_map/ppermute | solution.py:349
  22.0 1.4 %collective-permute-start.1 = (bf16[512,128]{1,0:T(8,128)(2,1)S(1)}, bf16[512,128]{1,0:T(8,128)(2,1)S(1)}, u32[]{:S(2)}, u32[]{:S(2)}) collective-permute-start(bf16[512,128]{1,0:T(8,128)(2,1)S(1)} %get-tuple-element.31), channel_id=1, source_target_pairs={{0,1},{1,0},{2,3},{3,2},{4,5},{5,4},{6,7},{7,6},{8,9},{9,8},{10,11... | collective-permute-start | bytes 393224 | tf_op jit(solution)/shard_map/ppermute | solution.py:349
  43.5 1.3 %collective-permute-start.2 = (bf16[512,128]{1,0:T(8,128)(2,1)S(1)}, bf16[512,128]{1,0:T(8,128)(2,1)S(1)}, u32[]{:S(2)}, u32[]{:S(2)}) collective-permute-start(bf16[512,128]{1,0:T(8,128)(2,1)S(1)} %bitcast.13), channel_id=1, source_target_pairs={{0,1},{1,0},{2,3},{3,2},{4,5},{5,4},{6,7},{7,6},{8,9},{9,8},{10,11... | collective-permute-start | bytes 393224 | tf_op jit(solution)/shard_map/ppermute | solution.py:349
  46.4 1.4 %collective-permute-start.3 = (bf16[512,128]{1,0:T(8,128)(2,1)S(1)}, bf16[512,128]{1,0:T(8,128)(2,1)S(1)}, u32[]{:S(2)}, u32[]{:S(2)}) collective-permute-start(bf16[512,128]{1,0:T(8,128)(2,1)S(1)} %get-tuple-element.48), channel_id=1, source_target_pairs={{0,1},{1,0},{2,3},{3,2},{4,5},{5,4},{6,7},{7,6},{8,9},{9,8},{10,11... | collective-permute-start | bytes 393224 | tf_op jit(solution)/shard_map/ppermute | solution.py:349

commit v8 on v7

--- a/solution.py
+++ b/solution.py
@@ -185,7 +185,7 @@
     return total.astype(BF16).astype(F32)
 
 
-def half_spread(ens_ref, slot, coeff, wide_ref, out_ref, tiles):
+def half_spread(ens_ref, slot, coeff, wide_ref, out_ref, tiles, send_ref=None):
     _, members, blocks, _ = ens_ref.shape
     rows, unroll = (8, 16) if coeff is None else (16, 8)
 
@@ -203,6 +203,9 @@
                 acc[t] = term if acc[t] is None else acc[t] + term
         for t in range(tiles):
             out_ref[pl.ds(first * tiles + t, rows, stride=tiles), :] = acc[t]
+        if send_ref is not None:
+            span = pl.ds(first * tiles, rows * tiles)
+            send_ref[span, :] = out_ref[span, :].astype(BF16)
 
     groups(blocks, rows, unroll, body)
 
@@ -211,8 +214,7 @@
     other[...] = other_ref[...].astype(F32)
     half_sums(ens_ref, 1, other, sums_ref, tiles, acc_ref)
     coeff_ref[...] = mixed(sums_ref[...], pad_ref, share_ref)
-    half_spread(ens_ref, 1, coeff_ref, wide_ref, spread, tiles)
-    send_ref[...] = spread[...].astype(BF16)
+    half_spread(ens_ref, 1, coeff_ref, wide_ref, spread, tiles, send_ref)
 
 
 def own_kernel(tiles, ens_ref, wide_ref, own_ref):
@@ -280,8 +282,7 @@
     sums = (beta + keep) * sums0_ref[...] - alpha * sums_ref[...]
     sums_ref[...] = sums
     coeff_ref[...] = mixed(sums, pad_ref, share_ref)
-    half_spread(ens_ref, 1, coeff_ref, wide_ref, spread, tiles)
-    send_ref[...] = spread[...].astype(BF16)
+    half_spread(ens_ref, 1, coeff_ref, wide_ref, spread, tiles, send_ref)
 
 
 def second_own_kernel(

time: 59.4 us -> 59.4 us (level)
  no operation moved by 1% of the time
where the time goes in v8:
time: 59.4 us; the launch traced here: 59 us
  blocking collectives  45.2 us (76%)
  Pallas kernels  9.69 us (16%)
  waiting for transfers between devices  1.31 us (2%)
  starting transfers between devices  1.03 us (2%)
  local copies, waits for them, and re-layouts  0.73 us (1%)
  between operations  0.73 us (1%)
    all_to_all x4, blocking collectives, exchange(): return lax.all_to_all(x, AXES, split_axis=0, concat_axis=0, tiled=True)  45.2 us
    pallas_call x1, Pallas kernels, per_device(): call(part(load_kernel, tiles), 'load', (shape((2, members, blocks, cells...  3.82 us
    pallas_call x1, Pallas kernels, per_device(): call(part(second_kernel, tiles), 'second', (to_swap, lanes, small, table,...  1.55 us
    pallas_call x1, Pallas kernels, per_device(): call(part(first_kernel, tiles), 'first', (to_swap, table, lanes, part_hal...  1.46 us
    ppermute x4, waiting for transfers between devices, swap(): return lax.ppermute(x, AXES, pairs)  1.31 us
  transfers between devices with their start and end apart: 4, of which 3 were waited for; matrix products, arithmetic and copies ran while one was open for 0% of the time, Pallas kernels for 10%

profile of v8, /device:TPU:1, one launch (start us, length us, event | category | flops | bytes accessed | tf_op | source)
XLA Modules:
  0.0 59.0 jit_solution(3828125143660046438)
XLA Ops:
  0.6 0.0 copy-start
  0.6 0.7 %copy-done = f32[4,1024]{1,0:T(4,128)S(1)} copy-done((f32[4,1024]{1,0:T(4,128)S(1)}, f32[4,1024]{1,0:T(4,128)}, u32[]{:S(2)}) %copy-start) | copy-done | bytes 16408
  1.4 15.1 %all_to_all.20 = bf16[32,16,128]{2,1,0:T(8,128)(2,1)S(1)} all-to-all(bf16[32,16,128]{2,1,0:T(8,128)(2,1)S(1)} %get-tuple-element.26), channel_id=1, replica_groups=mesh['mem'=4,'grid'=8] {'mem','grid'}, dimensions={0} | all-to-all | bytes 262144 | tf_op jit(solution)/shard_map/all_to_all | solution.py:353
  16.5 0.2 collective-permute-start
  16.7 3.8 %load.1 = (f32[2,32,128,512]{3,2,1,0:T(8,128)S(1)}, f32[7,128,128]{2,1,0:T(8,128)S(1)}, f32[128,128]{1,0:T(8,128)S(1)}, f32[32,128]{1,0:T(8,128)S(1)}, f32[512,128]{1,0:T(8,128)S(1)}) custom-call(bf16[32,128,1024]{2,1,0:T(8,128)(2,1)} %ens_hbm.1, s32[8,128]{1,0:T(8,128)} %bitcast.21, f32[8,128]{1,0:T(8,128)} %bitcast.22, f32[4,1024]{1,0:T(4,128)} %obs_hbm.1, ...), custom_call_target="tpu_custom_call" | custom-call | flops 8388608 | bytes 25165824 | tf_op jit(solution)/shard_map/load/pallas_call | solution.py:368
  20.5 0.0 collective-permute-done.other_ref
  20.5 1.5 %first.1 = (bf16[512,128]{1,0:T(8,128)(2,1)S(1)}, f32[128,128]{1,0:T(8,128)S(1)}, f32[32,128,128]{2,1,0:T(8,128)S(1)}, f32[512,128]{1,0:T(8,128)S(1)}) custom-call(f32[2,32,128,512]{3,2,1,0:T(8,128)S(1)} %get-tuple-element.27.ens_ref, f32[128,128]{1,0:T(8,128)S(1)} %get-tuple-element.28.acc_ref, bf16[512,128]{1,0:T(8,128)(2,1)S(1)} %collective-permute-done.other_ref, ...), custom_call_target="tpu_custom_call" | custom-call | flops 8388608 | tf_op jit(solution)/shard_map/first/pallas_call | solution.py:386
  22.0 0.4 collective-permute-start.1
  22.4 0.6 own.1
  23.0 0.5 collective-permute-done.1
  23.5 10.0 %all_to_all.21.got_ref = bf16[32,16,128]{2,1,0:T(8,128)(2,1)S(1)} all-to-all(bf16[32,16,128]{2,1,0:T(8,128)(2,1)S(1)} %bitcast.20), channel_id=1, replica_groups=mesh['mem'=4,'grid'=8] {'mem','grid'}, dimensions={0} | all-to-all | bytes 262144 | tf_op jit(solution)/shard_map/all_to_all | solution.py:353
  33.4 0.1 middle.1
  33.6 9.9 %all_to_all.22 = bf16[32,16,128]{2,1,0:T(8,128)(2,1)S(1)} all-to-all(bf16[32,16,128]{2,1,0:T(8,128)(2,1)S(1)} %get-tuple-element.34), channel_id=1, replica_groups=mesh['mem'=4,'grid'=8] {'mem','grid'}, dimensions={0} | all-to-all | bytes 262144 | tf_op jit(solution)/shard_map/all_to_all | solution.py:353
  43.5 0.2 collective-permute-start.2
  43.7 0.7 %sums.1 = (f32[128,128]{1,0:T(8,128)S(1)}, f32[128,128]{1,0:T(8,128)S(1)}, f32[128,128]{1,0:T(8,128)S(1)}, f32[128,128]{1,0:T(8,128)S(1)}) custom-call(f32[2,32,128,512]{3,2,1,0:T(8,128)S(1)} %get-tuple-element.27.ens_ref, bf16[512,128]{1,0:T(8,128)(2,1)S(1)} %bitcast.14, f32[512,128]{1,0:T(8,128)S(1)} %get-tuple-element.35.dm_ref, ...), custom_call_target="tpu_custom_call" | custom-call | flops 8388608 | tf_op jit(solution)/shard_map/sums/pallas_call | solution.py:398
  44.4 0.4 collective-permute-done.2.po_ref
  44.8 1.6 %second.1 = (bf16[512,128]{1,0:T(8,128)(2,1)S(1)}, f32[32,128,128]{2,1,0:T(8,128)S(1)}, f32[8,128]{1,0:T(8,128)S(1)}, f32[128,128]{1,0:T(8,128)S(1)}, f32[128,128]{1,0:T(8,128)S(1)}) custom-call(f32[2,32,128,512]{3,2,1,0:T(8,128)S(1)} %get-tuple-element.27.ens_ref, f32[128,128]{1,0:T(8,128)S(1)} %get-tuple-element.37.acc_ref, ...), custom_call_target="tpu_custom_call" | custom-call | flops 8388608 | tf_op jit(solution)/shard_map/second/pallas_call | solution.py:401
  46.4 0.3 collective-permute-start.3
  46.6 0.7 %second_own.1 = (f32[512,128]{1,0:T(8,128)S(1)}, f32[8,128]{1,0:T(8,128)S(1)}) custom-call(f32[2,32,128,512]{3,2,1,0:T(8,128)S(1)} %get-tuple-element.27.ens_ref, f32[32,128,128]{2,1,0:T(8,128)S(1)} %get-tuple-element.42.wide_ref, f32[128,128]{1,0:T(8,128)S(1)} %get-tuple-element.43.sums_ref, f32[128,128]{1,0:T(8,128)S(1)} %get-tuple-element.44.coeff_ref, ...), custom_call_target="tpu_custom_call" | custom-call | flops 8388608 | tf_op jit(solution)/shard_map/second_own/pallas_call | solution.py:410
  47.4 0.4 collective-permute-done.3
  47.8 0.2 pad_maximum_fusion
  48.0 10.1 %all_to_all.23 = bf16[32,9,2,128]{3,2,1,0:T(2,128)(2,1)S(1)} all-to-all(bf16[32,9,2,128]{3,2,1,0:T(2,128)(2,1)S(1)} %pad_maximum_fusion), channel_id=1, replica_groups=mesh['mem'=4,'grid'=8] {'mem','grid'}, dimensions={0} | all-to-all | bytes 294912 | tf_op jit(solution)/shard_map/all_to_all | solution.py:353
  58.2 0.1 convert_reduce_fusion
  58.3 0.7 %last.1 = (f32[4,1024]{1,0:T(4,128)}, f32[4,1024]{1,0:T(4,128)}) custom-call(f32[32,128]{1,0:T(8,128)S(1)} %bitcast.17, f32[2,2,128]{2,1,0:T(2,128)S(1)} %slice_bitcast_fusion.extra_ref, f32[8,128]{1,0:T(8,128)S(1)} %get-tuple-element.45.scal_ref, f32[32,128]{1,0:T(8,128)S(1)} %get-tuple-element.32.direct_ref, f32[32,128]{1,0:T(8,128)S(1)} %get-tuple-element.33.obs_ref, ...), custom_call_target="tpu_custom_call" | custom-call | tf_op jit(solution)/shard_map/last/pallas_call | solution.py:421
  (8 shorter events, 0.1 us)
Async XLA Ops:
  0.6 0.7 %copy-start = (f32[4,1024]{1,0:T(4,128)S(1)}, f32[4,1024]{1,0:T(4,128)}, u32[]{:S(2)}) copy-start(f32[4,1024]{1,0:T(4,128)} %right_ref.1) | copy-start | bytes 49156
  16.5 4.0 %collective-permute-start = (bf16[512,128]{1,0:T(8,128)(2,1)S(1)}, bf16[512,128]{1,0:T(8,128)(2,1)S(1)}, u32[]{:S(2)}, u32[]{:S(2)}) collective-permute-start(bf16[512,128]{1,0:T(8,128)(2,1)S(1)} %bitcast.15), channel_id=1, source_target_pairs={{0,1},{1,0},{2,3},{3,2},{4,5},{5,4},{6,7},{7,6},{8,9},{9,8},{10,11... | collective-permute-start | bytes 393224 | tf_op jit(solution)/shard_map/ppermute | solution.py:350
  22.0 1.4 %collective-permute-start.1 = (bf16[512,128]{1,0:T(8,128)(2,1)S(1)}, bf16[512,128]{1,0:T(8,128)(2,1)S(1)}, u32[]{:S(2)}, u32[]{:S(2)}) collective-permute-start(bf16[512,128]{1,0:T(8,128)(2,1)S(1)} %get-tuple-element.31), channel_id=1, source_target_pairs={{0,1},{1,0},{2,3},{3,2},{4,5},{5,4},{6,7},{7,6},{8,9},{9,8},{10,11... | collective-permute-start | bytes 393224 | tf_op jit(solution)/shard_map/ppermute | solution.py:350
  43.5 1.3 %collective-permute-start.2 = (bf16[512,128]{1,0:T(8,128)(2,1)S(1)}, bf16[512,128]{1,0:T(8,128)(2,1)S(1)}, u32[]{:S(2)}, u32[]{:S(2)}) collective-permute-start(bf16[512,128]{1,0:T(8,128)(2,1)S(1)} %bitcast.13), channel_id=1, source_target_pairs={{0,1},{1,0},{2,3},{3,2},{4,5},{5,4},{6,7},{7,6},{8,9},{9,8},{10,11... | collective-permute-start | bytes 393224 | tf_op jit(solution)/shard_map/ppermute | solution.py:350
  46.4 1.4 %collective-permute-start.3 = (bf16[512,128]{1,0:T(8,128)(2,1)S(1)}, bf16[512,128]{1,0:T(8,128)(2,1)S(1)}, u32[]{:S(2)}, u32[]{:S(2)}) collective-permute-start(bf16[512,128]{1,0:T(8,128)(2,1)S(1)} %get-tuple-element.48), channel_id=1, source_target_pairs={{0,1},{1,0},{2,3},{3,2},{4,5},{5,4},{6,7},{7,6},{8,9},{9,8},{10,11... | collective-permute-start | bytes 393224 | tf_op jit(solution)/shard_map/ppermute | solution.py:350

commit v9 on v8

--- a/solution.py
+++ b/solution.py
@@ -270,6 +270,7 @@
     dd = jnp.sum(dd_ref[...], axis=1, keepdims=True)
     pd = jnp.sum(pd_all[...], axis=1, keepdims=True)
     pp = jnp.sum(pp_all[...], axis=1, keepdims=True)
+    half_sums(ens_ref, 1, other, sums_ref, tiles, acc_ref)
     tau = jnp.where(dd > 0.0, (1.0 / KEEP - 1.0) * pd / jnp.where(dd > 0.0, dd, 1.0), 0.0)
     rr0 = jnp.sum(dd, axis=0, keepdims=True)
     alpha = rr0 / jnp.sum(pd + tau * dd, axis=0, keepdims=True)
@@ -278,7 +279,6 @@
     beta = rr1 / rr0
     row = lax.broadcasted_iota(jnp.int32, (8, LANES), 0)
     scal_ref[...] = jnp.where(row == 0, alpha, jnp.where(row == 1, beta, rr1))
-    half_sums(ens_ref, 1, other, sums_ref, tiles, acc_ref)
     sums = (beta + keep) * sums0_ref[...] - alpha * sums_ref[...]
     sums_ref[...] = sums
     coeff_ref[...] = mixed(sums, pad_ref, share_ref)

time: 59.4 us -> 59.4 us (level)
  no operation moved by 1% of the time
where the time goes in v9:
time: 59.4 us; the launch traced here: 59 us
  blocking collectives  45.2 us (76%)
  Pallas kernels  9.69 us (16%)
  waiting for transfers between devices  1.31 us (2%)
  starting transfers between devices  1.03 us (2%)
  local copies, waits for them, and re-layouts  0.73 us (1%)
  between operations  0.73 us (1%)
    all_to_all x4, blocking collectives, exchange(): return lax.all_to_all(x, AXES, split_axis=0, concat_axis=0, tiled=True)  45.2 us
    pallas_call x1, Pallas kernels, per_device(): call(part(load_kernel, tiles), 'load', (shape((2, members, blocks, cells...  3.82 us
    pallas_call x1, Pallas kernels, per_device(): call(part(second_kernel, tiles), 'second', (to_swap, lanes, small, table,...  1.55 us
    pallas_call x1, Pallas kernels, per_device(): call(part(first_kernel, tiles), 'first', (to_swap, table, lanes, part_hal...  1.46 us
    ppermute x4, waiting for transfers between devices, swap(): return lax.ppermute(x, AXES, pairs)  1.31 us
  transfers between devices with their start and end apart: 4, of which 3 were waited for; matrix products, arithmetic and copies ran while one was open for 0% of the time, Pallas kernels for 10%

profile of v9, /device:TPU:1, one launch (start us, length us, event | category | flops | bytes accessed | tf_op | source)
XLA Modules:
  0.0 59.0 jit_solution(937699233394433679)
XLA Ops:
  0.6 0.0 copy-start
  0.6 0.7 %copy-done = f32[4,1024]{1,0:T(4,128)S(1)} copy-done((f32[4,1024]{1,0:T(4,128)S(1)}, f32[4,1024]{1,0:T(4,128)}, u32[]{:S(2)}) %copy-start) | copy-done | bytes 16408
  1.4 15.1 %all_to_all.20 = bf16[32,16,128]{2,1,0:T(8,128)(2,1)S(1)} all-to-all(bf16[32,16,128]{2,1,0:T(8,128)(2,1)S(1)} %get-tuple-element.26), channel_id=1, replica_groups=mesh['mem'=4,'grid'=8] {'mem','grid'}, dimensions={0} | all-to-all | bytes 262144 | tf_op jit(solution)/shard_map/all_to_all | solution.py:353
  16.5 0.2 collective-permute-start
  16.7 3.8 %load.1 = (f32[2,32,128,512]{3,2,1,0:T(8,128)S(1)}, f32[7,128,128]{2,1,0:T(8,128)S(1)}, f32[128,128]{1,0:T(8,128)S(1)}, f32[32,128]{1,0:T(8,128)S(1)}, f32[512,128]{1,0:T(8,128)S(1)}) custom-call(bf16[32,128,1024]{2,1,0:T(8,128)(2,1)} %ens_hbm.1, s32[8,128]{1,0:T(8,128)} %bitcast.21, f32[8,128]{1,0:T(8,128)} %bitcast.22, f32[4,1024]{1,0:T(4,128)} %obs_hbm.1, ...), custom_call_target="tpu_custom_call" | custom-call | flops 8388608 | bytes 25165824 | tf_op jit(solution)/shard_map/load/pallas_call | solution.py:368
  20.5 0.0 collective-permute-done.other_ref
  20.5 1.5 %first.1 = (bf16[512,128]{1,0:T(8,128)(2,1)S(1)}, f32[128,128]{1,0:T(8,128)S(1)}, f32[32,128,128]{2,1,0:T(8,128)S(1)}, f32[512,128]{1,0:T(8,128)S(1)}) custom-call(f32[2,32,128,512]{3,2,1,0:T(8,128)S(1)} %get-tuple-element.27.ens_ref, f32[128,128]{1,0:T(8,128)S(1)} %get-tuple-element.28.acc_ref, bf16[512,128]{1,0:T(8,128)(2,1)S(1)} %collective-permute-done.other_ref, ...), custom_call_target="tpu_custom_call" | custom-call | flops 8388608 | tf_op jit(solution)/shard_map/first/pallas_call | solution.py:386
  22.0 0.4 collective-permute-start.1
  22.4 0.6 own.1
  23.0 0.5 collective-permute-done.1
  23.5 10.0 %all_to_all.21.got_ref = bf16[32,16,128]{2,1,0:T(8,128)(2,1)S(1)} all-to-all(bf16[32,16,128]{2,1,0:T(8,128)(2,1)S(1)} %bitcast.20), channel_id=1, replica_groups=mesh['mem'=4,'grid'=8] {'mem','grid'}, dimensions={0} | all-to-all | bytes 262144 | tf_op jit(solution)/shard_map/all_to_all | solution.py:353
  33.4 0.1 middle.1
  33.6 9.9 %all_to_all.22 = bf16[32,16,128]{2,1,0:T(8,128)(2,1)S(1)} all-to-all(bf16[32,16,128]{2,1,0:T(8,128)(2,1)S(1)} %get-tuple-element.34), channel_id=1, replica_groups=mesh['mem'=4,'grid'=8] {'mem','grid'}, dimensions={0} | all-to-all | bytes 262144 | tf_op jit(solution)/shard_map/all_to_all | solution.py:353
  43.5 0.2 collective-permute-start.2
  43.7 0.7 %sums.1 = (f32[128,128]{1,0:T(8,128)S(1)}, f32[128,128]{1,0:T(8,128)S(1)}, f32[128,128]{1,0:T(8,128)S(1)}, f32[128,128]{1,0:T(8,128)S(1)}) custom-call(f32[2,32,128,512]{3,2,1,0:T(8,128)S(1)} %get-tuple-element.27.ens_ref, bf16[512,128]{1,0:T(8,128)(2,1)S(1)} %bitcast.14, f32[512,128]{1,0:T(8,128)S(1)} %get-tuple-element.35.dm_ref, ...), custom_call_target="tpu_custom_call" | custom-call | flops 8388608 | tf_op jit(solution)/shard_map/sums/pallas_call | solution.py:398
  44.4 0.4 collective-permute-done.2.po_ref
  44.8 1.6 %second.1 = (bf16[512,128]{1,0:T(8,128)(2,1)S(1)}, f32[32,128,128]{2,1,0:T(8,128)S(1)}, f32[8,128]{1,0:T(8,128)S(1)}, f32[128,128]{1,0:T(8,128)S(1)}, f32[128,128]{1,0:T(8,128)S(1)}) custom-call(f32[2,32,128,512]{3,2,1,0:T(8,128)S(1)} %get-tuple-element.27.ens_ref, f32[128,128]{1,0:T(8,128)S(1)} %get-tuple-element.37.acc_ref, ...), custom_call_target="tpu_custom_call" | custom-call | flops 8388608 | tf_op jit(solution)/shard_map/second/pallas_call | solution.py:401
  46.4 0.3 collective-permute-start.3
  46.6 0.7 %second_own.1 = (f32[512,128]{1,0:T(8,128)S(1)}, f32[8,128]{1,0:T(8,128)S(1)}) custom-call(f32[2,32,128,512]{3,2,1,0:T(8,128)S(1)} %get-tuple-element.27.ens_ref, f32[32,128,128]{2,1,0:T(8,128)S(1)} %get-tuple-element.42.wide_ref, f32[128,128]{1,0:T(8,128)S(1)} %get-tuple-element.43.sums_ref, f32[128,128]{1,0:T(8,128)S(1)} %get-tuple-element.44.coeff_ref, ...), custom_call_target="tpu_custom_call" | custom-call | flops 8388608 | tf_op jit(solution)/shard_map/second_own/pallas_call | solution.py:410
  47.4 0.4 collective-permute-done.3
  47.8 0.2 pad_maximum_fusion
  48.0 10.1 %all_to_all.23 = bf16[32,9,2,128]{3,2,1,0:T(2,128)(2,1)S(1)} all-to-all(bf16[32,9,2,128]{3,2,1,0:T(2,128)(2,1)S(1)} %pad_maximum_fusion), channel_id=1, replica_groups=mesh['mem'=4,'grid'=8] {'mem','grid'}, dimensions={0} | all-to-all | bytes 294912 | tf_op jit(solution)/shard_map/all_to_all | solution.py:353
  58.2 0.1 convert_reduce_fusion
  58.3 0.7 %last.1 = (f32[4,1024]{1,0:T(4,128)}, f32[4,1024]{1,0:T(4,128)}) custom-call(f32[32,128]{1,0:T(8,128)S(1)} %bitcast.17, f32[2,2,128]{2,1,0:T(2,128)S(1)} %slice_bitcast_fusion.extra_ref, f32[8,128]{1,0:T(8,128)S(1)} %get-tuple-element.45.scal_ref, f32[32,128]{1,0:T(8,128)S(1)} %get-tuple-element.32.direct_ref, f32[32,128]{1,0:T(8,128)S(1)} %get-tuple-element.33.obs_ref, ...), custom_call_target="tpu_custom_call" | custom-call | tf_op jit(solution)/shard_map/last/pallas_call | solution.py:421
  (8 shorter events, 0.1 us)
Async XLA Ops:
  0.6 0.7 %copy-start = (f32[4,1024]{1,0:T(4,128)S(1)}, f32[4,1024]{1,0:T(4,128)}, u32[]{:S(2)}) copy-start(f32[4,1024]{1,0:T(4,128)} %right_ref.1) | copy-start | bytes 49156
  16.5 4.0 %collective-permute-start = (bf16[512,128]{1,0:T(8,128)(2,1)S(1)}, bf16[512,128]{1,0:T(8,128)(2,1)S(1)}, u32[]{:S(2)}, u32[]{:S(2)}) collective-permute-start(bf16[512,128]{1,0:T(8,128)(2,1)S(1)} %bitcast.15), channel_id=1, source_target_pairs={{0,1},{1,0},{2,3},{3,2},{4,5},{5,4},{6,7},{7,6},{8,9},{9,8},{10,11... | collective-permute-start | bytes 393224 | tf_op jit(solution)/shard_map/ppermute | solution.py:350
  22.0 1.4 %collective-permute-start.1 = (bf16[512,128]{1,0:T(8,128)(2,1)S(1)}, bf16[512,128]{1,0:T(8,128)(2,1)S(1)}, u32[]{:S(2)}, u32[]{:S(2)}) collective-permute-start(bf16[512,128]{1,0:T(8,128)(2,1)S(1)} %get-tuple-element.31), channel_id=1, source_target_pairs={{0,1},{1,0},{2,3},{3,2},{4,5},{5,4},{6,7},{7,6},{8,9},{9,8},{10,11... | collective-permute-start | bytes 393224 | tf_op jit(solution)/shard_map/ppermute | solution.py:350
  43.5 1.3 %collective-permute-start.2 = (bf16[512,128]{1,0:T(8,128)(2,1)S(1)}, bf16[512,128]{1,0:T(8,128)(2,1)S(1)}, u32[]{:S(2)}, u32[]{:S(2)}) collective-permute-start(bf16[512,128]{1,0:T(8,128)(2,1)S(1)} %bitcast.13), channel_id=1, source_target_pairs={{0,1},{1,0},{2,3},{3,2},{4,5},{5,4},{6,7},{7,6},{8,9},{9,8},{10,11... | collective-permute-start | bytes 393224 | tf_op jit(solution)/shard_map/ppermute | solution.py:350
  46.4 1.4 %collective-permute-start.3 = (bf16[512,128]{1,0:T(8,128)(2,1)S(1)}, bf16[512,128]{1,0:T(8,128)(2,1)S(1)}, u32[]{:S(2)}, u32[]{:S(2)}) collective-permute-start(bf16[512,128]{1,0:T(8,128)(2,1)S(1)} %get-tuple-element.48), channel_id=1, source_target_pairs={{0,1},{1,0},{2,3},{3,2},{4,5},{5,4},{6,7},{7,6},{8,9},{9,8},{10,11... | collective-permute-start | bytes 393224 | tf_op jit(solution)/shard_map/ppermute | solution.py:350
